TPU v7x, 128 devices: a whole 4x4x4 slice. The times are simulated.
128 devices in a mesh: lon: 16 (over x_lo, y, core), lat: 8 (over x_hi, z).
Axes of the slice: x: 4 (x_hi: 2, x_lo: 2; x = x_hi * 2 + x_lo), y: 4, z: 4, core: 2. Of those that a mesh axis runs over, the one named last changes fastest.
Arguments:
- radiances: bfloat16 [262144, 128], P(('lon', 'lat')), may hold values from -6 to 6
- owner_id: int32 [262144, 1], P(('lon', 'lat')), may hold values from 0 to 127; in each aligned block of 2048 rows (0 to 2047, 2048 to 4095, ...) at most 40 rows name the same one
- cell_index: int32 [262144, 4], P(('lon', 'lat')), may hold values from 0 to 6143
- valid_count: int32 [262144], P(('lon', 'lat')), may hold values from 1 to 4
- row_counts: int32 [128], P(('lon', 'lat')), may hold values from 1024 to 2048, as said below
- jacobian: bfloat16 [128, 96], replicated, may hold values from -0.5 to 0.5
- background: float32 [1536, 512, 96], P('lon', 'lat'), may hold values from -6 to 6
- vertical: float32 [96, 96], replicated, may hold values from -0.625 to 0.625
- lon_kernel: float32 [1536], replicated, may hold values from -0.15625 to 0.15625
Outputs:
- increment: float32 [1536, 512, 96], P('lon', 'lat')
Inputs may be any that keep to these rules, and one draw needn't show every extreme that they name: `owner_id`: among the rows of one ingestion list at most 40 name one owner, a bound that some block reaches. `row_counts`: at least half of 2048; some list is full.
All inputs are finite; a program needn't handle non-finite values.
Results may differ from a plain program's by a relative error of at most 0.0011.
Values may be sent and summed in bfloat16 or wider, within the bound.
No kernel may reach another device: no remote copies, remote signals or barrier semaphores. Data moves between devices by JAX's collectives and lax.ppermute only.
A program may use at most 128 MiB of HBM per device.

v0:
```python
import jax
import jax.numpy as jnp
from jax import lax
from jax.sharding import PartitionSpec as P


def circulant(doubled, length, first_row, nrows, ncols):
    begins = (length - 1 - (first_row + jnp.arange(nrows, dtype=jnp.int32))) % length
    return jax.vmap(lambda begin: lax.dynamic_slice_in_dim(doubled, begin, ncols))(begins)


def make_share(rows, counts, jacobian):
    profile = jnp.dot(rows, jacobian, preferred_element_type=jnp.float32)
    recip = 1.0 / jnp.maximum(counts, 1).astype(jnp.float32)
    return (profile * recip[:, None]).astype(jnp.bfloat16)


def rank_rows(owners, is_live, ndevices):
    rows_dev = owners.shape[0]
    block_rows = 256
    nblocks = rows_dev // block_rows
    owner_blocks = owners.reshape(nblocks, block_rows)
    live_blocks = is_live.reshape(nblocks, block_rows)
    lower = (jnp.arange(block_rows)[:, None] > jnp.arange(block_rows)[None, :]).astype(jnp.bfloat16)
    columns = jnp.arange(ndevices, dtype=jnp.int32)

    def step(carry, inputs):
        owner_part, live_part = inputs
        hits = (owner_part[:, None] == columns[None, :]) & live_part[:, None]
        hits_bf = hits.astype(jnp.bfloat16)
        before = jnp.dot(lower, hits_bf, preferred_element_type=jnp.float32) + carry[None, :]
        within = jnp.sum(jnp.where(hits, before, 0.0), axis=1)
        return (carry + jnp.sum(hits.astype(jnp.float32), axis=0), within)

    start = jnp.zeros((ndevices,), jnp.float32)
    _, within = lax.scan(step, start, (owner_blocks, live_blocks))
    return within.reshape(rows_dev).astype(jnp.int32)


def dispatch_rows(target, payload, extras, slots):
    block_slots = min(512, slots)
    nblocks = (slots + block_slots - 1) // block_slots
    starts = jnp.arange(nblocks, dtype=jnp.int32) * block_slots

    def dispatch_one_block(begin):
        slot_ids = begin + jnp.arange(block_slots, dtype=jnp.int32)
        picked = slot_ids[:, None] == target[None, :]
        rows_out = jnp.dot(picked.astype(jnp.bfloat16), payload, preferred_element_type=jnp.float32)
        extra_out = jnp.dot(
            picked.astype(jnp.float32),
            extras,
            precision=lax.Precision.HIGHEST,
            preferred_element_type=jnp.float32,
        )
        return (rows_out.astype(jnp.bfloat16), extra_out)

    rows_out, extra_out = lax.map(dispatch_one_block, starts)
    rows_out = rows_out.reshape(nblocks * block_slots, payload.shape[1])
    extra_out = extra_out.reshape(nblocks * block_slots, extras.shape[1])
    return (rows_out, extra_out)


def spread_forcing(share, got_cells, got_count, ncells):
    footprint = got_cells.shape[1]
    block_cells = min(512, ncells)
    nblocks = (ncells + block_cells - 1) // block_cells
    starts = jnp.arange(nblocks, dtype=jnp.int32) * block_cells
    masked = jnp.where(
        jnp.arange(footprint, dtype=jnp.int32)[None, :] < got_count[:, None], got_cells, -1
    )

    def spread_one_block(begin):
        cell_ids = begin + jnp.arange(block_cells, dtype=jnp.int32)
        hits = jnp.zeros((block_cells, masked.shape[0]), jnp.float32)
        for slot_number in range(footprint):
            hits = hits + (cell_ids[:, None] == masked[None, :, slot_number]).astype(jnp.float32)
        return jnp.dot(hits.astype(jnp.bfloat16), share, preferred_element_type=jnp.float32)

    forcing = lax.map(spread_one_block, starts)
    return forcing.reshape(nblocks * block_cells, share.shape[1])


def per_device(
    radiances,
    owner_id,
    cell_index,
    valid_count,
    row_counts,
    jacobian,
    background,
    vertical,
    lon_kernel,
):
    n_lon = lax.axis_size("lon")
    n_lat = lax.axis_size("lat")
    ndevices = n_lon * n_lat
    rows_dev = radiances.shape[0]
    footprint = cell_index.shape[1]
    capacity = max(2, 5 * rows_dev // (2 * ndevices))
    lon_dev, lat_dev, levels = background.shape
    ncells = lon_dev * lat_dev
    nlon = lon_kernel.shape[0]
    position = jnp.arange(rows_dev, dtype=jnp.int32)
    is_live = position < row_counts[0]
    owners = owner_id[:, 0]
    within = rank_rows(owners, is_live, ndevices)
    slots = ndevices * capacity
    target = jnp.where(is_live, owners * capacity + within, slots)
    extras = jnp.concatenate(
        [cell_index.astype(jnp.float32), valid_count.astype(jnp.float32)[:, None]], axis=1
    )
    send_rows, send_extra = dispatch_rows(target, radiances, extras, slots)
    send_cells = send_extra[:, :footprint].astype(jnp.int32)
    send_count = send_extra[:, footprint].astype(jnp.int32)
    got_rows, got_cells, got_count = (
        lax.all_to_all(send_rows, ("lon", "lat"), split_axis=0, concat_axis=0, tiled=True),
        lax.all_to_all(send_cells, ("lon", "lat"), split_axis=0, concat_axis=0, tiled=True),
        lax.all_to_all(send_count, ("lon", "lat"), split_axis=0, concat_axis=0, tiled=True),
    )
    share = lax.optimization_barrier(make_share(got_rows, got_count, jacobian))
    forcing = spread_forcing(share, got_cells, got_count, ncells)
    total = background.reshape(ncells, levels) + forcing
    mixed = jnp.dot(
        total, vertical.T, precision=lax.Precision.HIGHEST, preferred_element_type=jnp.float32
    )
    width = lat_dev * levels
    mixed = mixed.reshape(lon_dev, width)
    reversed_kernel = lon_kernel[::-1]
    doubled = jnp.concatenate([reversed_kernel, reversed_kernel])
    first_row = lax.axis_index("lon") * lon_dev
    piece = lax.all_gather(mixed, "lon", axis=0, tiled=True)
    block = circulant(doubled, nlon, first_row, lon_dev, piece.shape[0])
    result = jnp.dot(
        block, piece, precision=lax.Precision.HIGHEST, preferred_element_type=jnp.float32
    )
    return result.reshape(lon_dev, lat_dev, levels)


def solution(mesh):
    return jax.shard_map(
        per_device,
        mesh=mesh,
        in_specs=(
            P(("lon", "lat"), None),
            P(("lon", "lat"), None),
            P(("lon", "lat"), None),
            P(("lon", "lat")),
            P(("lon", "lat")),
            P(),
            P("lon", "lat", None),
            P(),
            P(),
        ),
        out_specs=P("lon", "lat", None),
        check_vma=False,
    )
```

profile of v0, /device:TPU:4, one launch (start us, length us, event | category | flops | bytes accessed | tf_op | source)
XLA Modules:
  0.0 442.3 jit_solution(10503805823642061901)
XLA Ops:
  7.1 1.3 fusion.45
  9.1 3.8 while.39
  12.9 0.8 convert_element_type.68
  14.5 56.0 %while.36 = (s32[]{:T(128)}, bf16[10,512,128]{2,1,0:T(8,128)(2,1)}, f32[10,512,5]{1,2,0:T(8,128)S(1)}, s32[10]{0:T(128)S(1)}, s32[2048]{0:T(1024)S(1)}, /*index=...) while((s32[]{:T(128)}, bf16[10,512,128]{2,1,0:T(8,128)(2,1)}, f32[10,512,5]{1,2,0:T(8,128)S(1)}, ...), condition=%wide.region_5.6_spmd, body=%wide.region_4.5_spmd.sunk | while | flops 333513216 | bytes 760425 | solution.py:57
  15.7 2.4 fusion.74
  18.2 1.9 fusion.75
  21.3 2.5 fusion.74
  23.8 1.9 fusion.75
  26.9 2.5 fusion.74
  29.4 1.9 fusion.75
  32.5 2.5 fusion.74
  35.0 1.9 fusion.75
  38.1 2.5 fusion.74
  40.6 1.9 fusion.75
  43.7 2.4 fusion.74
  46.2 1.9 fusion.75
  49.3 2.5 fusion.74
  51.7 1.9 fusion.75
  54.9 2.5 fusion.74
  57.4 1.9 fusion.75
  60.5 2.5 fusion.74
  63.0 1.9 fusion.75
  66.1 2.5 fusion.74
  68.5 1.9 fusion.75
  70.5 0.7 convert_element_type.71
  71.2 10.5 %all-to-all-start = ((s32[128,40,1]{1,2,0:T(1,128)}), s32[128,40,1]{1,2,0:T(1,128)S(1)}, u32[]{:S(2)}, u32[]{:S(2)}) async-start(s32[128,40,1]{1,2,0:T(1,128)} %bitcast.14), calls=%async_computation | async-start | bytes 131072 | tf_op jit(solution)/shard_map/all_to_all | solution.py:118
  82.1 0.9 reshape.146
  83.1 6.8 %all-to-all-done = s32[128,40,1]{1,2,0:T(1,128)S(1)} async-done(((s32[128,40,1]{1,2,0:T(1,128)}), s32[128,40,1]{1,2,0:T(1,128)S(1)}, u32[]{:S(2)}, u32[]{:S(2)}) %all-to-all-start) | async-done | bytes 20512 | tf_op jit(solution)/shard_map/all_to_all | solution.py:118
  89.9 5.7 %all-to-all-start.1 = ((s32[128,1,160]{2,1,0:T(1,128)}), s32[128,1,160]{2,1,0:T(1,128)S(1)}, u32[]{:S(2)}, u32[]{:S(2)}) async-start(s32[128,1,160]{2,1,0:T(1,128)} %reshape.146), calls=%async_computation.1 | async-start | bytes 262144 | tf_op jit(solution)/shard_map/all_to_all | solution.py:117
  95.6 0.8 reduce.13
  96.5 7.4 %all-to-all-done.1 = s32[128,1,160]{2,1,0:T(1,128)S(1)} async-done(((s32[128,1,160]{2,1,0:T(1,128)}), s32[128,1,160]{2,1,0:T(1,128)S(1)}, u32[]{:S(2)}, u32[]{:S(2)}) %all-to-all-start.1) | async-done | bytes 81952 | tf_op jit(solution)/shard_map/all_to_all | solution.py:117
  104.0 5.8 %all-to-all-start.2 = ((bf16[128,40,128]{2,1,0:T(8,128)(2,1)}), bf16[128,40,128]{2,1,0:T(8,128)(2,1)S(1)}, u32[]{:S(2)}, u32[]{:S(2)}) async-start(bf16[128,40,128]{2,1,0:T(8,128)(2,1)} %bitcast.15), calls=%async_computation.2 | async-start | bytes 2621440 | tf_op jit(solution)/shard_map/all_to_all | solution.py:116
  110.5 0.9 reduce.15
  111.9 18.5 %all-to-all-done.2 = bf16[128,40,128]{2,1,0:T(8,128)(2,1)S(1)} async-done(((bf16[128,40,128]{2,1,0:T(8,128)(2,1)}), bf16[128,40,128]{2,1,0:T(8,128)(2,1)S(1)}, u32[]{:S(2)}, u32[]{:S(2)}) %all-to-all-start.2) | async-done | bytes 1310752 | tf_op jit(solution)/shard_map/all_to_all | solution.py:116
  131.0 0.8 copy.22
  131.8 77.3 %while.37 = (s32[]{:T(128)}, f32[12,512,96]{1,2,0:T(8,128)}, s32[12]{0:T(128)S(1)}, s32[5120,4]{0,1:T(4,128)S(1)}, bf16[5120,96]{1,0:T(8,128)(2,1)S(1)}, /*index=5*/s32[]{:T(128)}) while((s32[]{:T(128)}, f32[12,512,96]{1,2,0:T(8,128)}, s32[12]{0:T(128)S(1)}, s32[5120,4]{0,1:T(4,128)S(1)}, bf16[5120,96]{1,0:T(8,128)(2,1)S(1)}, ...), condition=%wide.region_7.8_spmd, body=%wide.region_6.7_spmd.sunk | while | flops 534774272 | bytes 1430101 | solution.py:79
  133.2 5.0 %fusion.78 = f32[12,512,96]{1,2,0:T(8,128)} fusion(f32[12,512,96]{1,2,0:T(8,128)} %get-tuple-element.423, s32[]{:T(128)} %get-tuple-element.422, bf16[5120,96]{1,0:T(8,128)(2,1)S(1)} %get-tuple-element.432, s32[5120]{0:T(1024)S(1)} %bitcast.98, s32[5120]{0:T(1024)S(1)} %bitcast.99, s32[5120]{0:T(1024)S(1)} %bitcast.100, s32[5120]{0:T(1024)S(1)} %bitcast.97, ...), kind=kOutput, calls=%fused_computation.20.clone.1 | convolution fusion | flops 534773760 | bytes 1264128 | tf_op jit(solution)/shard_map/while/body/eval_jaxpr/dot_general | solution.py:77
  139.7 5.0 %fusion.78 = f32[12,512,96]{1,2,0:T(8,128)} fusion(f32[12,512,96]{1,2,0:T(8,128)} %get-tuple-element.423, s32[]{:T(128)} %get-tuple-element.422, bf16[5120,96]{1,0:T(8,128)(2,1)S(1)} %get-tuple-element.432, s32[5120]{0:T(1024)S(1)} %bitcast.98, s32[5120]{0:T(1024)S(1)} %bitcast.99, s32[5120]{0:T(1024)S(1)} %bitcast.100, s32[5120]{0:T(1024)S(1)} %bitcast.97, ...), kind=kOutput, calls=%fused_computation.20.clone.1 | convolution fusion | flops 534773760 | bytes 1264128 | tf_op jit(solution)/shard_map/while/body/eval_jaxpr/dot_general | solution.py:77
  146.1 5.0 %fusion.78 = f32[12,512,96]{1,2,0:T(8,128)} fusion(f32[12,512,96]{1,2,0:T(8,128)} %get-tuple-element.423, s32[]{:T(128)} %get-tuple-element.422, bf16[5120,96]{1,0:T(8,128)(2,1)S(1)} %get-tuple-element.432, s32[5120]{0:T(1024)S(1)} %bitcast.98, s32[5120]{0:T(1024)S(1)} %bitcast.99, s32[5120]{0:T(1024)S(1)} %bitcast.100, s32[5120]{0:T(1024)S(1)} %bitcast.97, ...), kind=kOutput, calls=%fused_computation.20.clone.1 | convolution fusion | flops 534773760 | bytes 1264128 | tf_op jit(solution)/shard_map/while/body/eval_jaxpr/dot_general | solution.py:77
  152.6 5.0 %fusion.78 = f32[12,512,96]{1,2,0:T(8,128)} fusion(f32[12,512,96]{1,2,0:T(8,128)} %get-tuple-element.423, s32[]{:T(128)} %get-tuple-element.422, bf16[5120,96]{1,0:T(8,128)(2,1)S(1)} %get-tuple-element.432, s32[5120]{0:T(1024)S(1)} %bitcast.98, s32[5120]{0:T(1024)S(1)} %bitcast.99, s32[5120]{0:T(1024)S(1)} %bitcast.100, s32[5120]{0:T(1024)S(1)} %bitcast.97, ...), kind=kOutput, calls=%fused_computation.20.clone.1 | convolution fusion | flops 534773760 | bytes 1264128 | tf_op jit(solution)/shard_map/while/body/eval_jaxpr/dot_general | solution.py:77
  159.0 5.0 %fusion.78 = f32[12,512,96]{1,2,0:T(8,128)} fusion(f32[12,512,96]{1,2,0:T(8,128)} %get-tuple-element.423, s32[]{:T(128)} %get-tuple-element.422, bf16[5120,96]{1,0:T(8,128)(2,1)S(1)} %get-tuple-element.432, s32[5120]{0:T(1024)S(1)} %bitcast.98, s32[5120]{0:T(1024)S(1)} %bitcast.99, s32[5120]{0:T(1024)S(1)} %bitcast.100, s32[5120]{0:T(1024)S(1)} %bitcast.97, ...), kind=kOutput, calls=%fused_computation.20.clone.1 | convolution fusion | flops 534773760 | bytes 1264128 | tf_op jit(solution)/shard_map/while/body/eval_jaxpr/dot_general | solution.py:77
  165.4 5.0 %fusion.78 = f32[12,512,96]{1,2,0:T(8,128)} fusion(f32[12,512,96]{1,2,0:T(8,128)} %get-tuple-element.423, s32[]{:T(128)} %get-tuple-element.422, bf16[5120,96]{1,0:T(8,128)(2,1)S(1)} %get-tuple-element.432, s32[5120]{0:T(1024)S(1)} %bitcast.98, s32[5120]{0:T(1024)S(1)} %bitcast.99, s32[5120]{0:T(1024)S(1)} %bitcast.100, s32[5120]{0:T(1024)S(1)} %bitcast.97, ...), kind=kOutput, calls=%fused_computation.20.clone.1 | convolution fusion | flops 534773760 | bytes 1264128 | tf_op jit(solution)/shard_map/while/body/eval_jaxpr/dot_general | solution.py:77
  171.9 5.0 %fusion.78 = f32[12,512,96]{1,2,0:T(8,128)} fusion(f32[12,512,96]{1,2,0:T(8,128)} %get-tuple-element.423, s32[]{:T(128)} %get-tuple-element.422, bf16[5120,96]{1,0:T(8,128)(2,1)S(1)} %get-tuple-element.432, s32[5120]{0:T(1024)S(1)} %bitcast.98, s32[5120]{0:T(1024)S(1)} %bitcast.99, s32[5120]{0:T(1024)S(1)} %bitcast.100, s32[5120]{0:T(1024)S(1)} %bitcast.97, ...), kind=kOutput, calls=%fused_computation.20.clone.1 | convolution fusion | flops 534773760 | bytes 1264128 | tf_op jit(solution)/shard_map/while/body/eval_jaxpr/dot_general | solution.py:77
  178.3 5.0 %fusion.78 = f32[12,512,96]{1,2,0:T(8,128)} fusion(f32[12,512,96]{1,2,0:T(8,128)} %get-tuple-element.423, s32[]{:T(128)} %get-tuple-element.422, bf16[5120,96]{1,0:T(8,128)(2,1)S(1)} %get-tuple-element.432, s32[5120]{0:T(1024)S(1)} %bitcast.98, s32[5120]{0:T(1024)S(1)} %bitcast.99, s32[5120]{0:T(1024)S(1)} %bitcast.100, s32[5120]{0:T(1024)S(1)} %bitcast.97, ...), kind=kOutput, calls=%fused_computation.20.clone.1 | convolution fusion | flops 534773760 | bytes 1264128 | tf_op jit(solution)/shard_map/while/body/eval_jaxpr/dot_general | solution.py:77
  184.8 5.0 %fusion.78 = f32[12,512,96]{1,2,0:T(8,128)} fusion(f32[12,512,96]{1,2,0:T(8,128)} %get-tuple-element.423, s32[]{:T(128)} %get-tuple-element.422, bf16[5120,96]{1,0:T(8,128)(2,1)S(1)} %get-tuple-element.432, s32[5120]{0:T(1024)S(1)} %bitcast.98, s32[5120]{0:T(1024)S(1)} %bitcast.99, s32[5120]{0:T(1024)S(1)} %bitcast.100, s32[5120]{0:T(1024)S(1)} %bitcast.97, ...), kind=kOutput, calls=%fused_computation.20.clone.1 | convolution fusion | flops 534773760 | bytes 1264128 | tf_op jit(solution)/shard_map/while/body/eval_jaxpr/dot_general | solution.py:77
  191.2 5.0 %fusion.78 = f32[12,512,96]{1,2,0:T(8,128)} fusion(f32[12,512,96]{1,2,0:T(8,128)} %get-tuple-element.423, s32[]{:T(128)} %get-tuple-element.422, bf16[5120,96]{1,0:T(8,128)(2,1)S(1)} %get-tuple-element.432, s32[5120]{0:T(1024)S(1)} %bitcast.98, s32[5120]{0:T(1024)S(1)} %bitcast.99, s32[5120]{0:T(1024)S(1)} %bitcast.100, s32[5120]{0:T(1024)S(1)} %bitcast.97, ...), kind=kOutput, calls=%fused_computation.20.clone.1 | convolution fusion | flops 534773760 | bytes 1264128 | tf_op jit(solution)/shard_map/while/body/eval_jaxpr/dot_general | solution.py:77
  197.6 5.0 %fusion.78 = f32[12,512,96]{1,2,0:T(8,128)} fusion(f32[12,512,96]{1,2,0:T(8,128)} %get-tuple-element.423, s32[]{:T(128)} %get-tuple-element.422, bf16[5120,96]{1,0:T(8,128)(2,1)S(1)} %get-tuple-element.432, s32[5120]{0:T(1024)S(1)} %bitcast.98, s32[5120]{0:T(1024)S(1)} %bitcast.99, s32[5120]{0:T(1024)S(1)} %bitcast.100, s32[5120]{0:T(1024)S(1)} %bitcast.97, ...), kind=kOutput, calls=%fused_computation.20.clone.1 | convolution fusion | flops 534773760 | bytes 1264128 | tf_op jit(solution)/shard_map/while/body/eval_jaxpr/dot_general | solution.py:77
  204.1 5.0 %fusion.78 = f32[12,512,96]{1,2,0:T(8,128)} fusion(f32[12,512,96]{1,2,0:T(8,128)} %get-tuple-element.423, s32[]{:T(128)} %get-tuple-element.422, bf16[5120,96]{1,0:T(8,128)(2,1)S(1)} %get-tuple-element.432, s32[5120]{0:T(1024)S(1)} %bitcast.98, s32[5120]{0:T(1024)S(1)} %bitcast.99, s32[5120]{0:T(1024)S(1)} %bitcast.100, s32[5120]{0:T(1024)S(1)} %bitcast.97, ...), kind=kOutput, calls=%fused_computation.20.clone.1 | convolution fusion | flops 534773760 | bytes 1264128 | tf_op jit(solution)/shard_map/while/body/eval_jaxpr/dot_general | solution.py:77
  209.1 2.2 copy.27
  211.3 2.6 bitcast_add_fusion
  213.9 2.6 fusion.46
  216.6 2.9 reshape.108
  219.6 140.5 %while.38 = (s32[]{:T(128)}, f32[3072]{0:T(1024)S(1)}, s32[96,1]{0,1:T(1,128)S(1)}, f32[96,1536]{1,0:T(8,128)S(1)}, s32[]{:T(128)}, /*index=5*/s32[]{:T(128)}) while((s32[]{:T(128)}, f32[3072]{0:T(1024)S(1)}, s32[96,1]{0,1:T(1,128)S(1)}, f32[96,1536]{1,0:T(8,128)S(1)}, s32[]{:T(128)}, /*index=5*/s32[]{:T(128)}) %tuple.72), condition=%wide.while_cond, body=%wide.while_body.sunk | while | flops 2 | bytes 36953 | solution.py:9
  226.0 0.7 dynamic-slice.7
  227.5 0.7 dynamic-slice.7
  255.3 0.7 dynamic-slice.7
  272.9 0.7 dynamic-slice.7
  275.8 0.7 dynamic-slice.7
  291.9 0.7 dynamic-slice.7
  294.8 0.7 dynamic-slice.7
  310.9 0.7 dynamic-slice.7
  360.1 47.1 %all-gather.2.cloned.1.call-done = f32[1536,6144]{1,0:T(8,128)} async-done(((f32[96,6144]{1,0:T(8,128)}), f32[1536,6144]{1,0:T(8,128)}) %all-gather.2.cloned.1.call-update) | async-done | bytes 37748752 | tf_op jit(solution)/shard_map/all_gather | solution.py:131
  407.2 25.8 %fusion.47 = f32[96,6144]{1,0:T(8,128)S(1)} fusion(f32[96,1536]{1,0:T(8,128)S(1)} %get-tuple-element.118, f32[1536,6144]{1,0:T(8,128)} %all-gather.2.cloned.1.call-done), kind=kOutput, calls=%fused_computation.62 | convolution fusion | flops 10871635968 | bytes 40697856 | tf_op jit(solution)/shard_map/dot_general | solution.py:133
  433.0 2.4 reshape.109
  (519 shorter events, 169.4 us)
Async XLA Ops:
  6.5 207.4 %copy-start = (f32[96,96]{1,0:T(8,128)S(1)}, f32[96,96]{1,0:T(8,128)}, u32[]{:S(2)}) copy-start(f32[96,96]{1,0:T(8,128)} %param.22) | copy-start | bytes 110596
  71.2 18.7 %all-to-all-start = ((s32[128,40,1]{1,2,0:T(1,128)}), s32[128,40,1]{1,2,0:T(1,128)S(1)}, u32[]{:S(2)}, u32[]{:S(2)}) async-start(s32[128,40,1]{1,2,0:T(1,128)} %bitcast.14), calls=%async_computation | async-start | bytes 131072 | tf_op jit(solution)/shard_map/all_to_all | solution.py:118
  81.7 48.7 %copy-start.1 = (bf16[128,96]{0,1:T(8,128)(2,1)S(1)}, bf16[128,96]{0,1:T(8,128)(2,1)}, u32[]{:S(2)}) copy-start(bf16[128,96]{0,1:T(8,128)(2,1)} %param.20) | copy-start | bytes 73732
  89.9 14.0 %all-to-all-start.1 = ((s32[128,1,160]{2,1,0:T(1,128)}), s32[128,1,160]{2,1,0:T(1,128)S(1)}, u32[]{:S(2)}, u32[]{:S(2)}) async-start(s32[128,1,160]{2,1,0:T(1,128)} %reshape.146), calls=%async_computation.1 | async-start | bytes 262144 | tf_op jit(solution)/shard_map/all_to_all | solution.py:117
  104.0 26.5 %all-to-all-start.2 = ((bf16[128,40,128]{2,1,0:T(8,128)(2,1)}), bf16[128,40,128]{2,1,0:T(8,128)(2,1)S(1)}, u32[]{:S(2)}, u32[]{:S(2)}) async-start(bf16[128,40,128]{2,1,0:T(8,128)(2,1)} %bitcast.15), calls=%async_computation.2 | async-start | bytes 2621440 | tf_op jit(solution)/shard_map/all_to_all | solution.py:116
  109.7 297.5 %all-gather.2.cloned.1.call-start = ((), (), s32[]{:S(2)}) async-start(), calls=%async_computation.3 | async-start | bytes 40108032 | tf_op jit(solution)/shard_map/all_gather | solution.py:131
  216.5 2.9 copy-start.2
Sparse Core Ops, SparseCore 0:
  219.6 187.5 all-gather.1
where the time goes:
time: 446 us; the launch traced here: 442 us
  local copies, waits for them, and re-layouts  166 us (37%)
  matrix products  134 us (30%)
  waiting for transfers between devices  79.9 us (18%)
  other arithmetic  22.9 us (5%)
  starting transfers between devices  22.2 us (5%)
  between operations  14.3 us (3%)
    gather x384, local copies, waits for them, and re-layouts  138 us
    dot_general x12, matrix products, spread_one_block(): jnp.dot(hits.astype(jnp.bfloat16), share, preferred_element_type=jnp.floa...  60.2 us
    all_gather x1, waiting for transfers between devices, per_device(): piece = lax.all_gather(mixed, 'lon', axis=0, tiled=True)  47.1 us
    dot_general x1, matrix products, per_device(): jnp.dot(block, piece, precision=lax.Precision.HIGHEST, preferred_element_...  25.8 us
    dot_general x10, matrix products, dispatch_one_block(): jnp.dot(picked.astype(jnp.bfloat16), payload, preferred_element_type=jnp....  24.6 us
    dot_general x10, matrix products, dispatch_one_block(): jnp.dot(picked.astype(jnp.float32), extras, precision=lax.Precision.HIGHE...  18.7 us
    all_to_all x1, waiting for transfers between devices, per_device(): lax.all_to_all(send_rows, ('lon', 'lat'), split_axis=0, concat_axis=0, ti...  18.5 us
    all_to_all x1, starting transfers between devices, per_device(): lax.all_to_all(send_count, ('lon', 'lat'), split_axis=0, concat_axis=0, t...  10.5 us
  transfers between devices with their start and end apart: 4, of which 4 were waited for; matrix products, arithmetic and copies ran while one was open for 32% of the time, Pallas kernels for 0%

commit v1 on v0

v1 whole, which is shorter than its diff:
```python
import jax
import jax.numpy as jnp
from jax import lax
from jax.experimental import pallas as pl
from jax.experimental.pallas import tpu as pltpu
from jax.sharding import PartitionSpec as P

F32 = jnp.float32
BF16 = jnp.bfloat16
I32 = jnp.int32
I16 = jnp.int16
LANES = 128
TOP = 32700.0
LOWEST = -110.0
CODE_ROWS = 8


def vmem(n):
    return [pl.BlockSpec(memory_space=pltpu.VMEM)] * n


def params():
    return pltpu.CompilerParams(vmem_limit_bytes=56 * 1024 * 1024)


def quantise(tiles, out_ref, place):
    rows = tiles[0].shape[0]
    for k, tile in enumerate(tiles):
        top = jnp.max(jnp.abs(tile), axis=0, keepdims=True)
        power = jnp.maximum(jnp.ceil(jnp.log2(top)), LOWEST)
        factor = jnp.exp2(-power) * TOP
        digits = jnp.round(tile * factor)
        codes = jnp.broadcast_to(power, (CODE_ROWS, LANES))
        whole = jnp.concatenate([digits, codes], axis=0).astype(I32)
        out_ref[place, :, k * LANES : (k + 1) * LANES] = whole.astype(I16)


def dequantise(in_ref, place):
    whole = in_ref[place].astype(I32).astype(F32)
    rows = whole.shape[0] - CODE_ROWS
    factor = jnp.exp2(whole[rows : rows + 1]) * (1.0 / TOP)
    return whole[:rows] * factor


def split(x):
    high = x.astype(BF16)
    low = (x - high.astype(F32)).astype(BF16)
    return high, low


def dispatch_kernel(
    capacity,
    live_ref,
    rad_ref,
    owner_ref,
    cell_ref,
    count_ref,
    jac_ref,
    out_ref,
    pay_ref,
    rows_ref,
    slot_v,
    slot_s,
    sem,
):
    nrows = rad_ref.shape[0]
    levels = jac_ref.shape[0]
    slots = out_ref.shape[0]
    ndev = slots // capacity
    foot = cell_ref.shape[0]
    n_live = live_ref[0]
    block = 256
    owner_ids = lax.broadcasted_iota(I32, (ndev, block), 0)
    earlier = (
        lax.broadcasted_iota(I32, (block, block), 0) < lax.broadcasted_iota(I32, (block, block), 1)
    ).astype(F32).astype(BF16)
    carry = jnp.zeros((ndev, 1), F32)
    for b in range(nrows // block):
        cols = slice(b * block, (b + 1) * block)
        position = lax.broadcasted_iota(I32, (1, block), 1) + b * block
        live = position < n_live
        owner = owner_ref[:, cols]
        hit = ((owner_ids == owner) & live).astype(F32)
        before = jnp.dot(hit.astype(BF16), earlier, preferred_element_type=F32) + carry
        rank = jnp.sum(hit * before, axis=0, keepdims=True).astype(I32)
        carry = carry + jnp.sum(hit, axis=1, keepdims=True)
        slot = jnp.where(live, owner * capacity + rank, slots)
        for i in range(block // LANES):
            row = b * (block // LANES) + i
            slot_v[row : row + 1, :] = slot[:, i * LANES : (i + 1) * LANES]
    copy = pltpu.make_async_copy(slot_v, slot_s, sem)
    copy.start()
    for b in range(nrows // block):
        cols = slice(b * block, (b + 1) * block)
        profile = lax.dot_general(
            jac_ref[...], rad_ref[cols, :], (((1,), (1,)), ((), ())), preferred_element_type=F32
        )
        count = count_ref[:, cols]
        share = (profile * (1.0 / count.astype(F32))).astype(BF16).astype(F32)
        cell = cell_ref[:, cols]
        used = lax.broadcasted_iota(I32, (foot, block), 0) < count
        lon = jnp.where(used, cell // 64, 0).astype(F32)
        lat = jnp.where(used, cell % 64, 64).astype(F32)
        rest = jnp.where(
            lax.broadcasted_iota(I32, (LANES - levels - 2 * foot, block), 0) == 0, 1.0, 0.0
        )
        payload = jnp.concatenate([share, jnp.concatenate([lon, lat], axis=0), rest], axis=0)
        pay_ref[cols, :] = payload.T
    rows_ref[...] = jnp.zeros_like(rows_ref)
    copy.wait()
    unroll = 16

    def move(c, _):
        for u in range(unroll):
            slot = slot_s[c // (LANES // unroll), (c % (LANES // unroll)) * unroll + u]
            rows_ref[pl.ds(slot, 1), :] = pay_ref[pl.ds(c * unroll + u, 1), :]
        return 0

    lax.fori_loop(0, (n_live + unroll - 1) // unroll, move, 0)
    out_ref[...] = rows_ref[:slots, :].astype(BF16)


def spread_kernel(
    capacity,
    lon_dev,
    lat_dev,
    got_ref,
    back_ref,
    vert_ref,
    out_ref,
    mix_ref,
    share_ref,
    acc0,
    acc1,
    acc2,
    acc3,
    meta_v,
    meta_s,
    sem,
):
    slots = got_ref.shape[0]
    levels = back_ref.shape[1]
    ndev = slots // capacity
    ncells = lon_dev * lat_dev
    foot = 4
    row_i = lax.broadcasted_iota(I32, (8, LANES), 0)
    lane_i = lax.broadcasted_iota(I32, (8, LANES), 1)
    is_foot = row_i < foot
    pick = jnp.where(is_foot & (lane_i == levels + row_i), 1.0, 0.0)
    pick = pick + jnp.where(is_foot & (lane_i == levels + foot + row_i), float(lon_dev), 0.0)
    pick = pick + jnp.where((row_i == foot) & (lane_i == levels + 2 * foot), 1.0, 0.0)
    pick = pick.astype(BF16)
    block = 512
    for b in range(slots // block):
        rows = slice(b * block, (b + 1) * block)
        part = got_ref[rows, :]
        meta = lax.dot_general(pick, part, (((1,), (1,)), ((), ())), preferred_element_type=F32)
        meta_v[:, rows] = meta.astype(I32)
        share_ref[rows, :] = part.astype(F32)
    copy = pltpu.make_async_copy(meta_v, meta_s, sem)
    copy.start()
    v_high, v_low = split(vert_ref[...])
    mix_ref[...] = jnp.zeros_like(mix_ref)
    mix_ref[:levels, :levels] = v_high
    mix_ref[:levels, LANES : LANES + levels] = v_high
    mix_ref[LANES : LANES + levels, :levels] = v_low
    for lat in range(lat_dev):
        acc0[lat * lon_dev : (lat + 1) * lon_dev, :levels] = back_ref[
            pl.ds(lat, lon_dev, stride=lat_dev), :
        ]
    accs = (acc0, acc1, acc2, acc3)
    for acc in accs[1:]:
        acc[...] = jnp.zeros_like(acc)
    copy.wait()
    chunk = 8

    def one_source(s, _):
        base = s * capacity
        n_chunks = meta_s[foot, base]
        for c in range(1, capacity // chunk):
            n_chunks = n_chunks + meta_s[foot, base + c * chunk]

        def one_chunk(c, _):
            first = base + c * chunk
            for u in range(chunk):
                row = share_ref[pl.ds(first + u, 1), :]
                for f in range(foot):
                    cell = meta_s[f, first + u]
                    accs[f][pl.ds(cell, 1), :] = accs[f][pl.ds(cell, 1), :] + row
            return 0

        lax.fori_loop(0, n_chunks, one_chunk, 0)
        return 0

    lax.fori_loop(0, ndev, one_source, 0)
    lane = lax.broadcasted_iota(I32, (lon_dev, LANES), 1)
    real = lax.broadcasted_iota(I32, (4 * lon_dev, LANES), 1) < levels

    def one_group(t, _):
        rows = pl.ds(pl.multiple_of(t * 4 * lon_dev, 4 * lon_dev), 4 * lon_dev)
        total = (acc0[rows, :] + acc1[rows, :]) + (acc2[rows, :] + acc3[rows, :])
        total = jnp.where(real, total, 0.0)
        high, low = split(total)
        both = lax.dot_general(
            jnp.concatenate([high, low], axis=1),
            mix_ref[...],
            (((1,), (1,)), ((), ())),
            preferred_element_type=F32,
        )
        mixed = both[:, :LANES] + both[:, LANES:]
        a = [mixed[j * lon_dev : (j + 1) * lon_dev, :] for j in range(4)]
        r1 = pltpu.roll(a[1], 96, 1)
        r2 = pltpu.roll(a[2], 64, 1)
        r3 = pltpu.roll(a[3], 32, 1)
        tiles = [
            jnp.where(lane < 96, a[0], r1),
            jnp.where(lane < 64, r1, r2),
            jnp.where(lane < 32, r2, r3),
        ]
        quantise(tiles, out_ref, t)
        return 0

    lax.fori_loop(0, ncells // (4 * lon_dev), one_group, 0)


def toeplitz_kernel(kern_ref, ph_ref, pl_ref, mh_ref, ml_ref):
    n = kern_ref.shape[1]
    block = 256
    for high_ref, low_ref, row, sign in ((ph_ref, pl_ref, 0, False), (mh_ref, ml_ref, 1, True)):
        base = jnp.broadcast_to(kern_ref[row : row + 1, :], (block, n))
        strip = pltpu.roll(base, 0, 1, stride=1, stride_axis=0)
        for i in range(n // block):
            if i:
                strip = jnp.concatenate([strip[:, n - block :], strip[:, : n - block]], axis=1)
            piece = strip
            if sign:
                row_i = lax.broadcasted_iota(I32, (block, n), 0) + i * block
                piece = jnp.where(lax.broadcasted_iota(I32, (block, n), 1) > row_i, -strip, strip)
            high, low = split(piece)
            high_ref[i * block : (i + 1) * block, :] = high
            low_ref[i * block : (i + 1) * block, :] = low


def conv_kernel(got_ref, ph_ref, pl_ref, mh_ref, ml_ref, out_ref, xph, xpl, xmh, xml, yp, ym):
    n_lon = got_ref.shape[0]
    rows = got_ref.shape[1] - CODE_ROWS
    half = n_lon // 2
    for s in range(half):
        a = dequantise(got_ref, s)
        b = dequantise(got_ref, s + half)
        at = slice(s * rows, (s + 1) * rows)
        xph[at, :], xpl[at, :] = split(a + b)
        xmh[at, :], xml[at, :] = split(a - b)
    for th, tl, xh, xl, y in ((ph_ref, pl_ref, xph, xpl, yp), (mh_ref, ml_ref, xmh, xml, ym)):
        y[...] = (
            jnp.dot(th[...], xh[...], preferred_element_type=F32)
            + jnp.dot(tl[...], xh[...], preferred_element_type=F32)
            + jnp.dot(th[...], xl[...], preferred_element_type=F32)
        )
    width = got_ref.shape[2]
    for s in range(half):
        at = slice(s * rows, (s + 1) * rows)
        plus, minus = yp[at, :], ym[at, :]
        for place, y in ((s, 0.5 * (plus + minus)), (s + half, 0.5 * (plus - minus))):
            quantise([y[:, k : k + LANES] for k in range(0, width, LANES)], out_ref, place)


def unpack_kernel(lat_dev, got_ref, out_ref):
    n_lon = got_ref.shape[0]
    lon_dev = got_ref.shape[1] - CODE_ROWS
    levels = out_ref.shape[1]
    lane = lax.broadcasted_iota(I32, (lon_dev, LANES), 1)
    for t in range(n_lon):
        x = dequantise(got_ref, t)
        o = [x[:, k * LANES : (k + 1) * LANES] for k in range(3)]
        a = [
            o[0],
            pltpu.roll(jnp.where(lane >= 96, o[0], o[1]), 32, 1),
            pltpu.roll(jnp.where(lane >= 64, o[1], o[2]), 64, 1),
            pltpu.roll(o[2], 96, 1),
        ]
        for j in range(4):
            out_ref[pl.ds(t * 4 + j, lon_dev, stride=lat_dev), :] = a[j][:, :levels]


def per_device(
    radiances,
    owner_id,
    cell_index,
    valid_count,
    row_counts,
    jacobian,
    background,
    vertical,
    lon_kernel,
):
    n_lon = lax.axis_size("lon")
    ndev = n_lon * lax.axis_size("lat")
    nrows = radiances.shape[0]
    lon_dev, lat_dev, levels = background.shape
    capacity = 5 * nrows // (2 * ndev)
    slots = ndev * capacity
    ncells = lon_dev * lat_dev
    width = ncells // n_lon // lon_dev * levels
    coded = (n_lon, lon_dev + CODE_ROWS, width)

    sent = pl.pallas_call(
        lambda *refs: dispatch_kernel(capacity, *refs),
        out_shape=jax.ShapeDtypeStruct((slots, LANES), BF16),
        in_specs=[pl.BlockSpec(memory_space=pltpu.SMEM)] + vmem(5),
        out_specs=vmem(1)[0],
        scratch_shapes=[
            pltpu.VMEM((nrows, LANES), F32),
            pltpu.VMEM((slots + 8, LANES), F32),
            pltpu.VMEM((nrows // LANES, LANES), I32),
            pltpu.SMEM((nrows // LANES, LANES), I32),
            pltpu.SemaphoreType.DMA,
        ],
        compiler_params=params(),
        name="dispatch",
    )(
        row_counts,
        radiances,
        owner_id.T,
        cell_index.T,
        valid_count.reshape(1, nrows),
        jacobian.T,
    )
    got = lax.all_to_all(
        sent.reshape(ndev, capacity, LANES), ("lon", "lat"), split_axis=0, concat_axis=0, tiled=True
    ).reshape(slots, LANES)

    acc = pltpu.VMEM((ncells + 8, LANES), F32)
    field = pl.pallas_call(
        lambda *refs: spread_kernel(capacity, lon_dev, lat_dev, *refs),
        out_shape=jax.ShapeDtypeStruct(coded, I16),
        in_specs=vmem(3),
        out_specs=vmem(1)[0],
        scratch_shapes=[
            pltpu.VMEM((2 * LANES, 2 * LANES), BF16),
            pltpu.VMEM((slots, LANES), F32),
            acc,
            acc,
            acc,
            acc,
            pltpu.VMEM((8, slots), I32),
            pltpu.SMEM((8, slots), I32),
            pltpu.SemaphoreType.DMA,
        ],
        compiler_params=params(),
        name="spread",
    )(got, background.reshape(ncells, levels), vertical)

    half = n_lon * lon_dev // 2
    turned_kernel = jnp.roll(lon_kernel[::-1], 1)
    plus = turned_kernel[:half] + turned_kernel[half:]
    minus = turned_kernel[half:] - turned_kernel[:half]
    first = lon_kernel[:half] - lon_kernel[half:]
    minus = jnp.roll(first[::-1], 1)
    square = jax.ShapeDtypeStruct((half, half), BF16)
    toeplitz = pl.pallas_call(
        toeplitz_kernel,
        out_shape=(square,) * 4,
        in_specs=vmem(1),
        out_specs=tuple(vmem(4)),
        compiler_params=params(),
        name="toeplitz",
    )(jnp.stack([plus, minus]))

    columns = lax.all_to_all(field, "lon", split_axis=0, concat_axis=0, tiled=True)
    part = pltpu.VMEM((half, width), BF16)
    wide = pltpu.VMEM((half, width), F32)
    result = pl.pallas_call(
        conv_kernel,
        out_shape=jax.ShapeDtypeStruct(coded, I16),
        in_specs=vmem(5),
        out_specs=vmem(1)[0],
        scratch_shapes=[part, part, part, part, wide, wide],
        compiler_params=params(),
        name="convolve",
    )(columns, *toeplitz)
    back = lax.all_to_all(result, "lon", split_axis=0, concat_axis=0, tiled=True)
    out = pl.pallas_call(
        lambda *refs: unpack_kernel(lat_dev, *refs),
        out_shape=jax.ShapeDtypeStruct((ncells, levels), F32),
        in_specs=vmem(1),
        out_specs=vmem(1)[0],
        compiler_params=params(),
        name="unpack",
    )(back)
    return out.reshape(lon_dev, lat_dev, levels)


def solution(mesh):
    return jax.shard_map(
        per_device,
        mesh=mesh,
        in_specs=(
            P(("lon", "lat"), None),
            P(("lon", "lat"), None),
            P(("lon", "lat"), None),
            P(("lon", "lat")),
            P(("lon", "lat")),
            P(),
            P("lon", "lat", None),
            P(),
            P(),
        ),
        out_specs=P("lon", "lat", None),
        check_vma=False,
    )
```

time: 446 us -> 146 us (0.33)
  local copies, waits for them, and re-layouts: 166 us -> 2.71 us
  matrix products: 134 us -> 0 us
  Pallas kernels: 0 us -> 68.7 us
  waiting for transfers between devices: 79.9 us -> 12.2 us
  blocking collectives: 0 us -> 54.8 us
  other arithmetic: 22.9 us -> 2.07 us
  starting transfers between devices: 22.2 us -> 3.71 us
  between operations: 14.3 us -> 0.7 us
    gather x384 -> x0, local copies, waits for them, and re-layouts: 138 us -> none
    dot_general x43 -> x0, matrix products: 134 us -> none  [the longest x12 60.2 us: spread_one_block(): jnp.dot(hits.astype(jnp.bfloat16), share, preferred_element_type=jnp.floa...]
    pallas_call x0 -> x5, Pallas kernels: none -> 68.7 us  [the longest x1 43 us: per_device(): pl.pallas_call(lambda *refs: spread_kernel(capacity, lon_dev, lat_dev, *r...]
    all_to_all x0 -> x2, blocking collectives: none -> 54.8 us  [the longest x1 31.4 us: per_device(): lax.all_to_all(sent.reshape(ndev, capacity, LANES), ('lon', 'lat'), split...]
    all_gather x1 -> x0, waiting for transfers between devices: 47.1 us -> none  [per_device(): piece = lax.all_gather(mixed, 'lon', axis=0, tiled=True)]
    all_to_all x3 -> x1, waiting for transfers between devices: 32.8 us -> 12.2 us  [per_device(): lax.all_to_all(field, 'lon', split_axis=0, concat_axis=0, tiled=True)]
    all_to_all x3 -> x1, starting transfers between devices: 22 us -> 3.71 us  [per_device(): lax.all_to_all(field, 'lon', split_axis=0, concat_axis=0, tiled=True)]
    add x31 -> x1, other arithmetic: 17.2 us -> 0.76 us  [per_device(): plus = turned_kernel[:half] + turned_kernel[half:]]
  transfers between devices with their start and end apart: 4 -> 1, of which waited for: 4 -> 1; matrix products, arithmetic and copies ran while one was open for 32% -> 3% of each run, Pallas kernels for 0% -> 2%
where the time goes in v1:
time: 146 us; the launch traced here: 145 us
  Pallas kernels  68.7 us (47%)
  blocking collectives  54.8 us (38%)
  waiting for transfers between devices  12.2 us (8%)
  starting transfers between devices  3.71 us (3%)
  local copies, waits for them, and re-layouts  2.71 us (2%)
  other arithmetic  2.07 us (1%)
    pallas_call x1, Pallas kernels, per_device(): pl.pallas_call(lambda *refs: spread_kernel(capacity, lon_dev, lat_dev, *r...  43 us
    all_to_all x1, blocking collectives, per_device(): lax.all_to_all(sent.reshape(ndev, capacity, LANES), ('lon', 'lat'), split...  31.4 us
    all_to_all x1, blocking collectives, per_device(): lax.all_to_all(result, 'lon', split_axis=0, concat_axis=0, tiled=True)  23.3 us
    all_to_all x1, waiting for transfers between devices, per_device(): lax.all_to_all(field, 'lon', split_axis=0, concat_axis=0, tiled=True)  12.2 us
    pallas_call x1, Pallas kernels, per_device(): pl.pallas_call(conv_kernel, out_shape=jax.ShapeDtypeStruct(coded, I16), i...  8.3 us
    pallas_call x1, Pallas kernels, per_device(): pl.pallas_call(lambda *refs: dispatch_kernel(capacity, *refs), out_shape=...  8.26 us
    pallas_call x1, Pallas kernels, per_device(): pl.pallas_call(lambda *refs: unpack_kernel(lat_dev, *refs), out_shape=jax...  5.97 us
    all_to_all x1, starting transfers between devices, per_device(): lax.all_to_all(field, 'lon', split_axis=0, concat_axis=0, tiled=True)  3.71 us
  transfers between devices with their start and end apart: 1, of which 1 were waited for; matrix products, arithmetic and copies ran while one was open for 3% of the time, Pallas kernels for 2%

profile of v1, /device:TPU:4, one launch (start us, length us, event | category | flops | bytes accessed | tf_op | source)
XLA Modules:
  0.0 144.9 jit_solution(12920679943502661784)
XLA Ops:
  0.7 8.3 %dispatch.1 = bf16[5120,128]{1,0:T(8,128)(2,1)} custom-call(s32[1]{0:T(128)S(6)} %copy.10.refs_0_, bf16[2048,128]{1,0:T(8,128)(2,1)} %refs_1_.1, s32[1,2048]{1,0:T(1,128)} %bitcast.17, s32[4,2048]{1,0:T(4,128)} %bitcast.13, s32[1,2048]{1,0:T(1,128)} %bitcast.18, bf16[96,128]{1,0:T(8,128)(2,1)} %bitcast.15), custom_call_target="tpu_custom_call" | custom-call | tf_op jit(solution)/shard_map/dispatch/pallas_call | solution.py:307
  8.9 31.4 %all_to_all.15 = bf16[128,40,128]{2,1,0:T(8,128)(2,1)} all-to-all(bf16[128,40,128]{2,1,0:T(8,128)(2,1)} %bitcast.10), channel_id=1, replica_groups=mesh['lon'=16,'lat'=8] {'lon','lat'}, dimensions={0} | all-to-all | bytes 2621440 | tf_op jit(solution)/shard_map/all_to_all | solution.py:329
  40.4 43.0 %spread.1 = s16[16,104,384]{2,1,0:T(8,128)(2,1)} custom-call(bf16[5120,128]{1,0:T(8,128)(2,1)} %bitcast.11, f32[6144,96]{1,0:T(8,128)} %bitcast.12, f32[96,96]{1,0:T(8,128)} %refs_2_.1), custom_call_target="tpu_custom_call" | custom-call | tf_op jit(solution)/shard_map/spread/pallas_call | solution.py:334
  83.4 0.0 copy-start.1
  83.4 3.7 %all-to-all-start.1 = ((s16[16,104,384]{2,1,0:T(8,128)(2,1)}), s16[16,104,384]{2,1,0:T(8,128)(2,1)S(1)}, u32[]{:S(2)}, u32[]{:S(2)}) async-start(s16[16,104,384]{2,1,0:T(8,128)(2,1)} %spread.1), calls=%async_computation.1 | async-start | bytes 2555904 | tf_op jit(solution)/shard_map/all_to_all | solution.py:370
  87.1 0.0 copy-done.1
  87.2 0.6 slice.41
  87.7 0.1 slice.42
  87.8 0.1 fusion.1
  87.9 0.5 slice.49
  88.4 0.1 slice.50
  88.5 0.1 reverse.6
  88.6 0.1 slice.55
  88.6 0.1 slice.46
  88.7 0.8 fusion
  89.5 0.1 reverse.5
  89.6 0.1 slice.54
  89.7 0.6 pad_maximum_fusion.2
  90.3 0.6 pad_maximum_fusion.kern_ref
  90.9 3.1 %toeplitz.1 = (bf16[768,768]{1,0:T(8,128)(2,1)}, bf16[768,768]{1,0:T(8,128)(2,1)}, bf16[768,768]{1,0:T(8,128)(2,1)}, bf16[768,768]{1,0:T(8,128)(2,1)}) custom-call(f32[2,768]{1,0:T(2,128)} %pad_maximum_fusion.kern_ref), custom_call_target="tpu_custom_call" | custom-call | tf_op jit(solution)/shard_map/toeplitz/pallas_call | solution.py:361
  94.0 12.2 %all-to-all-done.1.got_ref = s16[16,104,384]{2,1,0:T(8,128)(2,1)S(1)} async-done(((s16[16,104,384]{2,1,0:T(8,128)(2,1)}), s16[16,104,384]{2,1,0:T(8,128)(2,1)S(1)}, u32[]{:S(2)}, u32[]{:S(2)}) %all-to-all-start.1) | async-done | bytes 1277984 | tf_op jit(solution)/shard_map/all_to_all | solution.py:370
  106.2 0.0 copy-start
  106.2 1.0 copy-done
  107.3 8.3 %convolve.1 = s16[16,104,384]{2,1,0:T(8,128)(2,1)} custom-call(s16[16,104,384]{2,1,0:T(8,128)(2,1)} %copy-done, bf16[768,768]{1,0:T(8,128)(2,1)} %get-tuple-element.9.ph_ref, bf16[768,768]{1,0:T(8,128)(2,1)} %get-tuple-element.10.pl_ref, bf16[768,768]{1,0:T(8,128)(2,1)} %get-tuple-element.11.mh_ref, bf16[768,768]{1,0:T(8,128)(2,1)} %get-tuple-element.12.ml_ref), custom_call_target="tpu_custom_call" | custom-call | tf_op jit(solution)/shard_map/convolve/pallas_call | solution.py:373
  115.6 23.3 %all_to_all.16.refs_0_ = s16[16,104,384]{2,1,0:T(8,128)(2,1)} all-to-all(s16[16,104,384]{2,1,0:T(8,128)(2,1)} %convolve.1), channel_id=1, replica_groups=mesh['lon'=16,'lat'=8] {'lon'}, dimensions={0} | all-to-all | bytes 2555904 | tf_op jit(solution)/shard_map/all_to_all | solution.py:382
  138.9 6.0 %unpack.1 = f32[6144,96]{1,0:T(8,128)} custom-call(s16[16,104,384]{2,1,0:T(8,128)(2,1)} %all_to_all.16.refs_0_), custom_call_target="tpu_custom_call" | custom-call | tf_op jit(solution)/shard_map/unpack/pallas_call | solution.py:383
  (2 shorter events, 0.0 us)
Async XLA Ops:
  83.4 3.7 %copy-start.1 = (f32[1536]{0:T(1024)S(1)}, f32[1536]{0:T(1024)}, u32[]{:S(2)}) copy-start(f32[1536]{0:T(1024)} %param.17) | copy-start | bytes 18436
  83.4 22.8 %all-to-all-start.1 = ((s16[16,104,384]{2,1,0:T(8,128)(2,1)}), s16[16,104,384]{2,1,0:T(8,128)(2,1)S(1)}, u32[]{:S(2)}, u32[]{:S(2)}) async-start(s16[16,104,384]{2,1,0:T(8,128)(2,1)} %spread.1), calls=%async_computation.1 | async-start | bytes 2555904 | tf_op jit(solution)/shard_map/all_to_all | solution.py:370
  106.2 1.0 copy-start

commit v2 on v1

--- a/solution.py
+++ b/solution.py
@@ -58,7 +58,8 @@
     jac_ref,
     out_ref,
     pay_ref,
-    rows_ref,
+    even_ref,
+    odd_ref,
     slot_v,
     slot_s,
     sem,
@@ -106,29 +107,31 @@
         )
         payload = jnp.concatenate([share, jnp.concatenate([lon, lat], axis=0), rest], axis=0)
         pay_ref[cols, :] = payload.T
-    rows_ref[...] = jnp.zeros_like(rows_ref)
+    even_ref[...] = jnp.zeros_like(even_ref)
+    odd_ref[...] = jnp.zeros_like(odd_ref)
     copy.wait()
     unroll = 16
 
     def move(c, _):
         for u in range(unroll):
             slot = slot_s[c // (LANES // unroll), (c % (LANES // unroll)) * unroll + u]
-            rows_ref[pl.ds(slot, 1), :] = pay_ref[pl.ds(c * unroll + u, 1), :]
+            to_ref = odd_ref if u % 2 else even_ref
+            to_ref[pl.ds(slot, 1), :] = pay_ref[pl.ds(c * unroll + u, 1), :]
         return 0
 
     lax.fori_loop(0, (n_live + unroll - 1) // unroll, move, 0)
-    out_ref[...] = rows_ref[:slots, :].astype(BF16)
+    out_ref[...] = (even_ref[:slots, :] + odd_ref[:slots, :]).astype(BF16)
 
 
 def spread_kernel(
     capacity,
     lon_dev,
     lat_dev,
+    levels,
     got_ref,
     back_ref,
-    vert_ref,
+    mix_ref,
     out_ref,
-    mix_ref,
     share_ref,
     acc0,
     acc1,
@@ -136,13 +139,14 @@
     acc3,
     meta_v,
     meta_s,
-    sem,
+    sems,
 ):
     slots = got_ref.shape[0]
-    levels = back_ref.shape[1]
     ndev = slots // capacity
     ncells = lon_dev * lat_dev
     foot = 4
+    load = pltpu.make_async_copy(back_ref, acc0.at[pl.ds(0, ncells), :], sems.at[0])
+    load.start()
     row_i = lax.broadcasted_iota(I32, (8, LANES), 0)
     lane_i = lax.broadcasted_iota(I32, (8, LANES), 1)
     is_foot = row_i < foot
@@ -157,20 +161,12 @@
         meta = lax.dot_general(pick, part, (((1,), (1,)), ((), ())), preferred_element_type=F32)
         meta_v[:, rows] = meta.astype(I32)
         share_ref[rows, :] = part.astype(F32)
-    copy = pltpu.make_async_copy(meta_v, meta_s, sem)
+    copy = pltpu.make_async_copy(meta_v, meta_s, sems.at[1])
     copy.start()
-    v_high, v_low = split(vert_ref[...])
-    mix_ref[...] = jnp.zeros_like(mix_ref)
-    mix_ref[:levels, :levels] = v_high
-    mix_ref[:levels, LANES : LANES + levels] = v_high
-    mix_ref[LANES : LANES + levels, :levels] = v_low
-    for lat in range(lat_dev):
-        acc0[lat * lon_dev : (lat + 1) * lon_dev, :levels] = back_ref[
-            pl.ds(lat, lon_dev, stride=lat_dev), :
-        ]
     accs = (acc0, acc1, acc2, acc3)
     for acc in accs[1:]:
         acc[...] = jnp.zeros_like(acc)
+    load.wait()
     copy.wait()
     chunk = 8
 
@@ -194,18 +190,13 @@
 
     lax.fori_loop(0, ndev, one_source, 0)
     lane = lax.broadcasted_iota(I32, (lon_dev, LANES), 1)
-    real = lax.broadcasted_iota(I32, (4 * lon_dev, LANES), 1) < levels
 
     def one_group(t, _):
         rows = pl.ds(pl.multiple_of(t * 4 * lon_dev, 4 * lon_dev), 4 * lon_dev)
         total = (acc0[rows, :] + acc1[rows, :]) + (acc2[rows, :] + acc3[rows, :])
-        total = jnp.where(real, total, 0.0)
         high, low = split(total)
-        both = lax.dot_general(
-            jnp.concatenate([high, low], axis=1),
-            mix_ref[...],
-            (((1,), (1,)), ((), ())),
-            preferred_element_type=F32,
+        both = jnp.dot(
+            jnp.concatenate([high, low], axis=1), mix_ref[...], preferred_element_type=F32
         )
         mixed = both[:, :LANES] + both[:, LANES:]
         a = [mixed[j * lon_dev : (j + 1) * lon_dev, :] for j in range(4)]
@@ -220,7 +211,22 @@
         quantise(tiles, out_ref, t)
         return 0
 
-    lax.fori_loop(0, ncells // (4 * lon_dev), one_group, 0)
+    lax.fori_loop(0, ncells // (4 * lon_dev), one_group, 0, unroll=4)
+
+
+def prepare_kernel(lat_dev, back_ref, vert_ref, out_ref, mix_ref):
+    ncells, levels = back_ref.shape
+    lon_dev = ncells // lat_dev
+    v_high, v_low = split(vert_ref[...])
+    mix_ref[...] = jnp.zeros_like(mix_ref)
+    mix_ref[:levels, :levels] = v_high
+    mix_ref[:levels, LANES : LANES + levels] = v_low
+    mix_ref[LANES : LANES + levels, :levels] = v_high
+    out_ref[...] = jnp.zeros_like(out_ref)
+    for lat in range(lat_dev):
+        out_ref[lat * lon_dev : (lat + 1) * lon_dev, :levels] = back_ref[
+            pl.ds(lat, lon_dev, stride=lat_dev), :
+        ]
 
 
 def toeplitz_kernel(kern_ref, ph_ref, pl_ref, mh_ref, ml_ref):
@@ -241,7 +247,12 @@
             low_ref[i * block : (i + 1) * block, :] = low
 
 
-def conv_kernel(got_ref, ph_ref, pl_ref, mh_ref, ml_ref, out_ref, xph, xpl, xmh, xml, yp, ym):
+def conv_kernel(got_ref, *refs):
+    hbm, out_ref, held, (xph, xpl, xmh, xml, yp, ym, sems) = refs[:4], refs[4], refs[5:9], refs[9:]
+    loads = [pltpu.make_async_copy(a, b, sems.at[i]) for i, (a, b) in enumerate(zip(hbm, held))]
+    for load in loads:
+        load.start()
+    ph_ref, pl_ref, mh_ref, ml_ref = held
     n_lon = got_ref.shape[0]
     rows = got_ref.shape[1] - CODE_ROWS
     half = n_lon // 2
@@ -251,6 +262,8 @@
         at = slice(s * rows, (s + 1) * rows)
         xph[at, :], xpl[at, :] = split(a + b)
         xmh[at, :], xml[at, :] = split(a - b)
+    for load in loads:
+        load.wait()
     for th, tl, xh, xl, y in ((ph_ref, pl_ref, xph, xpl, yp), (mh_ref, ml_ref, xmh, xml, ym)):
         y[...] = (
             jnp.dot(th[...], xh[...], preferred_element_type=F32)
@@ -265,12 +278,11 @@
             quantise([y[:, k : k + LANES] for k in range(0, width, LANES)], out_ref, place)
 
 
-def unpack_kernel(lat_dev, got_ref, out_ref):
-    n_lon = got_ref.shape[0]
-    lon_dev = got_ref.shape[1] - CODE_ROWS
-    levels = out_ref.shape[1]
+def unpack_kernel(got_ref, out_ref):
+    lon_dev, lats, levels = out_ref.shape
     lane = lax.broadcasted_iota(I32, (lon_dev, LANES), 1)
-    for t in range(n_lon):
+    flat = out_ref.reshape(lon_dev * lats, levels)
+    for t in range(got_ref.shape[0]):
         x = dequantise(got_ref, t)
         o = [x[:, k * LANES : (k + 1) * LANES] for k in range(3)]
         a = [
@@ -280,7 +292,7 @@
             pltpu.roll(o[2], 96, 1),
         ]
         for j in range(4):
-            out_ref[pl.ds(t * 4 + j, lon_dev, stride=lat_dev), :] = a[j][:, :levels]
+            flat[pl.ds(t * 4 + j, lon_dev, stride=lats), :] = a[j][:, :levels]
 
 
 def per_device(
@@ -312,6 +324,7 @@
         scratch_shapes=[
             pltpu.VMEM((nrows, LANES), F32),
             pltpu.VMEM((slots + 8, LANES), F32),
+            pltpu.VMEM((slots + 8, LANES), F32),
             pltpu.VMEM((nrows // LANES, LANES), I32),
             pltpu.SMEM((nrows // LANES, LANES), I32),
             pltpu.SemaphoreType.DMA,
@@ -326,18 +339,29 @@
         valid_count.reshape(1, nrows),
         jacobian.T,
     )
+    sent, background, turned = lax.optimization_barrier((sent, background, vertical.T))
     got = lax.all_to_all(
         sent.reshape(ndev, capacity, LANES), ("lon", "lat"), split_axis=0, concat_axis=0, tiled=True
     ).reshape(slots, LANES)
-
+    ordered, mixer = pl.pallas_call(
+        lambda *refs: prepare_kernel(lat_dev, *refs),
+        out_shape=(
+            jax.ShapeDtypeStruct((ncells, LANES), F32),
+            jax.ShapeDtypeStruct((2 * LANES, 2 * LANES), BF16),
+        ),
+        in_specs=vmem(2),
+        out_specs=tuple(vmem(2)),
+        compiler_params=params(),
+        cost_estimate=pl.CostEstimate(flops=0, bytes_accessed=12_000_000, transcendentals=0),
+        name="prepare",
+    )(background.reshape(ncells, levels), turned)
     acc = pltpu.VMEM((ncells + 8, LANES), F32)
     field = pl.pallas_call(
-        lambda *refs: spread_kernel(capacity, lon_dev, lat_dev, *refs),
+        lambda *refs: spread_kernel(capacity, lon_dev, lat_dev, levels, *refs),
         out_shape=jax.ShapeDtypeStruct(coded, I16),
-        in_specs=vmem(3),
+        in_specs=[vmem(1)[0], pl.BlockSpec(memory_space=pl.ANY), vmem(1)[0]],
         out_specs=vmem(1)[0],
         scratch_shapes=[
-            pltpu.VMEM((2 * LANES, 2 * LANES), BF16),
             pltpu.VMEM((slots, LANES), F32),
             acc,
             acc,
@@ -345,11 +369,11 @@
             acc,
             pltpu.VMEM((8, slots), I32),
             pltpu.SMEM((8, slots), I32),
-            pltpu.SemaphoreType.DMA,
+            pltpu.SemaphoreType.DMA((2,)),
         ],
         compiler_params=params(),
         name="spread",
-    )(got, background.reshape(ncells, levels), vertical)
+    )(got, ordered, mixer)
 
     half = n_lon * lon_dev // 2
     turned_kernel = jnp.roll(lon_kernel[::-1], 1)
@@ -373,22 +397,25 @@
     result = pl.pallas_call(
         conv_kernel,
         out_shape=jax.ShapeDtypeStruct(coded, I16),
-        in_specs=vmem(5),
+        in_specs=vmem(1) + [pl.BlockSpec(memory_space=pl.ANY)] * 4,
         out_specs=vmem(1)[0],
-        scratch_shapes=[part, part, part, part, wide, wide],
+        scratch_shapes=[pltpu.VMEM((half, half), BF16)] * 4
+        + [part] * 4
+        + [wide] * 2
+        + [pltpu.SemaphoreType.DMA((4,))],
         compiler_params=params(),
         name="convolve",
     )(columns, *toeplitz)
     back = lax.all_to_all(result, "lon", split_axis=0, concat_axis=0, tiled=True)
-    out = pl.pallas_call(
-        lambda *refs: unpack_kernel(lat_dev, *refs),
-        out_shape=jax.ShapeDtypeStruct((ncells, levels), F32),
-        in_specs=vmem(1),
-        out_specs=vmem(1)[0],
+    return pl.pallas_call(
+        unpack_kernel,
+        grid=(n_lon // 2,),
+        out_shape=jax.ShapeDtypeStruct((lon_dev, lat_dev, levels), F32),
+        in_specs=[pl.BlockSpec((2,) + coded[1:], lambda g: (g, 0, 0))],
+        out_specs=pl.BlockSpec((lon_dev, 8, levels), lambda g: (0, g, 0)),
         compiler_params=params(),
         name="unpack",
     )(back)
-    return out.reshape(lon_dev, lat_dev, levels)
 
 
 def solution(mesh):

time: 146 us -> 142 us (0.973)
  blocking collectives: 54.8 us -> 23.4 us
  starting transfers between devices: 3.71 us -> 30.9 us
  Pallas kernels: 68.7 us -> 51.8 us
  waiting for transfers between devices: 12.2 us -> 27 us
  local copies, waits for them, and re-layouts: 2.71 us -> 5.23 us
    all_to_all x1 -> x0, blocking collectives: 31.4 us -> none  [per_device(): lax.all_to_all(sent.reshape(ndev, capacity, LANES), ('lon', 'lat'), split...]
    pallas_call x2 -> x3, Pallas kernels: 49 us -> 31.4 us  [the longest x1 19.3 us: per_device(): pl.pallas_call(lambda *refs: spread_kernel(capacity, lon_dev, lat_dev, le...]
    all_to_all x1, starting transfers between devices: 3.71 us -> 19.7 us  [per_device(): lax.all_to_all(field, 'lon', split_axis=0, concat_axis=0, tiled=True)]
    all_to_all x0 -> x1, waiting for transfers between devices: none -> 14.7 us  [per_device(): lax.all_to_all(sent.reshape(ndev, capacity, LANES), ('lon', 'lat'), split...]
    all_to_all x0 -> x1, starting transfers between devices: none -> 11.2 us  [per_device(): lax.all_to_all(sent.reshape(ndev, capacity, LANES), ('lon', 'lat'), split...]
    unnamed x8 -> x11, local copies, waits for them, and re-layouts: 1.37 us -> 3.95 us
  transfers between devices with their start and end apart: 1 -> 2, of which waited for: 1 -> 2; matrix products, arithmetic and copies ran while one was open for 3% -> 3% of each run, Pallas kernels for 2% -> 6%
where the time goes in v2:
time: 142 us; the launch traced here: 141 us
  Pallas kernels  51.8 us (36%)
  starting transfers between devices  30.9 us (22%)
  waiting for transfers between devices  27 us (19%)
  blocking collectives  23.4 us (16%)
  local copies, waits for them, and re-layouts  5.23 us (4%)
  other arithmetic  2.1 us (1%)
    all_to_all x1, blocking collectives, per_device(): lax.all_to_all(result, 'lon', split_axis=0, concat_axis=0, tiled=True)  23.4 us
    all_to_all x1, starting transfers between devices, per_device(): lax.all_to_all(field, 'lon', split_axis=0, concat_axis=0, tiled=True)  19.7 us
    pallas_call x1, Pallas kernels, per_device(): pl.pallas_call(lambda *refs: spread_kernel(capacity, lon_dev, lat_dev, le...  19.3 us
    all_to_all x1, waiting for transfers between devices, per_device(): lax.all_to_all(sent.reshape(ndev, capacity, LANES), ('lon', 'lat'), split...  14.7 us
    all_to_all x1, waiting for transfers between devices, per_device(): lax.all_to_all(field, 'lon', split_axis=0, concat_axis=0, tiled=True)  12.3 us
    all_to_all x1, starting transfers between devices, per_device(): lax.all_to_all(sent.reshape(ndev, capacity, LANES), ('lon', 'lat'), split...  11.2 us
    pallas_call x1, Pallas kernels, per_device(): pl.pallas_call(conv_kernel, out_shape=jax.ShapeDtypeStruct(coded, I16), i...  8.98 us
    pallas_call x1, Pallas kernels, per_device(): pl.pallas_call(lambda *refs: dispatch_kernel(capacity, *refs), out_shape=...  8.32 us
  transfers between devices with their start and end apart: 2, of which 2 were waited for; matrix products, arithmetic and copies ran while one was open for 3% of the time, Pallas kernels for 6%

profile of v2, /device:TPU:4, one launch (start us, length us, event | category | flops | bytes accessed | tf_op | source)
XLA Modules:
  0.0 141.1 jit_solution(14786584635408979795)
XLA Ops:
  0.7 1.5 %copy.10 = f32[96,96]{0,1:T(8,128)} copy(f32[96,96]{1,0:T(8,128)} %param.16) | data formatting | bytes 73728 | tf_op args[7]
  2.2 8.3 %dispatch.1 = bf16[5120,128]{1,0:T(8,128)(2,1)} custom-call(s32[1]{0:T(128)S(6)} %copy.11.refs_0_, bf16[2048,128]{1,0:T(8,128)(2,1)} %refs_1_.1, s32[1,2048]{1,0:T(1,128)} %bitcast.18, s32[4,2048]{1,0:T(4,128)} %bitcast.14, s32[1,2048]{1,0:T(1,128)} %bitcast.19, bf16[96,128]{1,0:T(8,128)(2,1)} %bitcast.16), custom_call_target="tpu_custom_call" | custom-call | tf_op jit(solution)/shard_map/dispatch/pallas_call | solution.py:319
  10.5 11.2 %all-to-all-start = ((bf16[128,40,128]{2,1,0:T(8,128)(2,1)}), bf16[128,40,128]{2,1,0:T(8,128)(2,1)S(1)}, u32[]{:S(2)}, u32[]{:S(2)}) async-start(bf16[128,40,128]{2,1,0:T(8,128)(2,1)} %bitcast.10), calls=%async_computation | async-start | bytes 2621440 | tf_op jit(solution)/shard_map/all_to_all | solution.py:343
  21.7 5.9 %prepare.1 = (f32[6144,128]{1,0:T(8,128)}, bf16[256,256]{1,0:T(8,128)(2,1)}) custom-call(f32[6144,96]{1,0:T(8,128)} %bitcast.12, f32[96,96]{1,0:T(8,128)} %bitcast.13), custom_call_target="tpu_custom_call" | custom-call | bytes 12000000 | tf_op jit(solution)/shard_map/prepare/pallas_call | solution.py:346
  27.6 14.7 %all-to-all-done = bf16[128,40,128]{2,1,0:T(8,128)(2,1)S(1)} async-done(((bf16[128,40,128]{2,1,0:T(8,128)(2,1)}), bf16[128,40,128]{2,1,0:T(8,128)(2,1)S(1)}, u32[]{:S(2)}, u32[]{:S(2)}) %all-to-all-start) | async-done | bytes 1310752 | tf_op jit(solution)/shard_map/all_to_all | solution.py:343
  42.4 0.0 copy-start
  42.4 1.1 copy-done
  43.5 19.3 %spread.1 = s16[16,104,384]{2,1,0:T(8,128)(2,1)} custom-call(bf16[5120,128]{1,0:T(8,128)(2,1)} %bitcast.11, f32[6144,128]{1,0:T(8,128)} %get-tuple-element.17.refs_1_, bf16[256,256]{1,0:T(8,128)(2,1)} %get-tuple-element.18.refs_2_), custom_call_target="tpu_custom_call" | custom-call | tf_op jit(solution)/shard_map/spread/pallas_call | solution.py:359
  62.8 0.0 copy-start.2
  62.8 19.7 %all-to-all-start.1 = ((s16[16,104,384]{2,1,0:T(8,128)(2,1)}), s16[16,104,384]{2,1,0:T(8,128)(2,1)S(1)}, u32[]{:S(2)}, u32[]{:S(2)}) async-start(s16[16,104,384]{2,1,0:T(8,128)(2,1)} %spread.1), calls=%async_computation.1 | async-start | bytes 2555904 | tf_op jit(solution)/shard_map/all_to_all | solution.py:394
  82.5 0.0 copy-done.2
  82.5 0.5 slice.41
  83.0 0.1 slice.42
  83.1 0.1 fusion.1
  83.1 0.5 slice.49
  83.7 0.1 slice.50
  83.7 0.1 reverse.6
  83.8 0.1 slice.55
  83.9 0.1 slice.46
  84.0 0.7 fusion
  84.7 0.1 reverse.5
  84.8 0.1 slice.54
  84.8 0.7 pad_maximum_fusion.2
  85.6 0.6 pad_maximum_fusion.kern_ref
  86.2 3.1 %toeplitz.1 = (bf16[768,768]{1,0:T(8,128)(2,1)}, bf16[768,768]{1,0:T(8,128)(2,1)}, bf16[768,768]{1,0:T(8,128)(2,1)}, bf16[768,768]{1,0:T(8,128)(2,1)}) custom-call(f32[2,768]{1,0:T(2,128)} %pad_maximum_fusion.kern_ref), custom_call_target="tpu_custom_call" | custom-call | tf_op jit(solution)/shard_map/toeplitz/pallas_call | solution.py:385
  89.3 12.3 %all-to-all-done.1.got_ref = s16[16,104,384]{2,1,0:T(8,128)(2,1)S(1)} async-done(((s16[16,104,384]{2,1,0:T(8,128)(2,1)}), s16[16,104,384]{2,1,0:T(8,128)(2,1)S(1)}, u32[]{:S(2)}, u32[]{:S(2)}) %all-to-all-start.1) | async-done | bytes 1277984 | tf_op jit(solution)/shard_map/all_to_all | solution.py:394
  101.6 0.0 copy-start.1
  101.6 1.0 copy-done.1
  102.6 9.0 %convolve.1 = s16[16,104,384]{2,1,0:T(8,128)(2,1)} custom-call(s16[16,104,384]{2,1,0:T(8,128)(2,1)} %copy-done.1, bf16[768,768]{1,0:T(8,128)(2,1)} %get-tuple-element.19.refs_0_, bf16[768,768]{1,0:T(8,128)(2,1)} %get-tuple-element.20.refs_1_, bf16[768,768]{1,0:T(8,128)(2,1)} %get-tuple-element.21.refs_2_, bf16[768,768]{1,0:T(8,128)(2,1)} %get-tuple-element.22.refs_3_), custom_call_target="tpu_custom_call" | custom-call | tf_op jit(solution)/shard_map/convolve/pallas_call | solution.py:397
  111.6 23.4 %all_to_all.15.got_ref = s16[16,104,384]{2,1,0:T(8,128)(2,1)} all-to-all(s16[16,104,384]{2,1,0:T(8,128)(2,1)} %convolve.1), channel_id=1, replica_groups=mesh['lon'=16,'lat'=8] {'lon'}, dimensions={0} | all-to-all | bytes 2555904 | tf_op jit(solution)/shard_map/all_to_all | solution.py:409
  135.0 6.2 %unpack.1 = f32[96,64,96]{2,1,0:T(8,128)} custom-call(s16[16,104,384]{2,1,0:T(8,128)(2,1)} %all_to_all.15.got_ref), custom_call_target="tpu_custom_call" | custom-call | tf_op jit(solution)/shard_map/unpack/pallas_call | solution.py:410
  (2 shorter events, 0.0 us)
Async XLA Ops:
  10.5 31.9 %all-to-all-start = ((bf16[128,40,128]{2,1,0:T(8,128)(2,1)}), bf16[128,40,128]{2,1,0:T(8,128)(2,1)S(1)}, u32[]{:S(2)}, u32[]{:S(2)}) async-start(bf16[128,40,128]{2,1,0:T(8,128)(2,1)} %bitcast.10), calls=%async_computation | async-start | bytes 2621440 | tf_op jit(solution)/shard_map/all_to_all | solution.py:343
  42.4 1.1 copy-start
  62.8 19.7 %copy-start.2 = (f32[1536]{0:T(1024)S(1)}, f32[1536]{0:T(1024)}, u32[]{:S(2)}) copy-start(f32[1536]{0:T(1024)} %param.17) | copy-start | bytes 18436
  62.8 38.8 %all-to-all-start.1 = ((s16[16,104,384]{2,1,0:T(8,128)(2,1)}), s16[16,104,384]{2,1,0:T(8,128)(2,1)S(1)}, u32[]{:S(2)}, u32[]{:S(2)}) async-start(s16[16,104,384]{2,1,0:T(8,128)(2,1)} %spread.1), calls=%async_computation.1 | async-start | bytes 2555904 | tf_op jit(solution)/shard_map/all_to_all | solution.py:394
  101.6 1.0 copy-start.1

commit v3 on v2

--- a/solution.py
+++ b/solution.py
@@ -88,8 +88,8 @@
         slot = jnp.where(live, owner * capacity + rank, slots)
         for i in range(block // LANES):
             row = b * (block // LANES) + i
-            slot_v[row : row + 1, :] = slot[:, i * LANES : (i + 1) * LANES]
-    copy = pltpu.make_async_copy(slot_v, slot_s, sem)
+            slot_v[:, row * LANES : (row + 1) * LANES] = slot[:, i * LANES : (i + 1) * LANES]
+    copy = pltpu.make_async_copy(slot_v.at[0], slot_s, sem)
     copy.start()
     for b in range(nrows // block):
         cols = slice(b * block, (b + 1) * block)
@@ -114,7 +114,7 @@
 
     def move(c, _):
         for u in range(unroll):
-            slot = slot_s[c // (LANES // unroll), (c % (LANES // unroll)) * unroll + u]
+            slot = slot_s[c * unroll + u]
             to_ref = odd_ref if u % 2 else even_ref
             to_ref[pl.ds(slot, 1), :] = pay_ref[pl.ds(c * unroll + u, 1), :]
         return 0
@@ -137,9 +137,10 @@
     acc1,
     acc2,
     acc3,
+    fields_v,
     meta_v,
-    meta_s,
     sems,
+    *tables,
 ):
     slots = got_ref.shape[0]
     ndev = slots // capacity
@@ -147,45 +148,63 @@
     foot = 4
     load = pltpu.make_async_copy(back_ref, acc0.at[pl.ds(0, ncells), :], sems.at[0])
     load.start()
-    row_i = lax.broadcasted_iota(I32, (8, LANES), 0)
-    lane_i = lax.broadcasted_iota(I32, (8, LANES), 1)
-    is_foot = row_i < foot
-    pick = jnp.where(is_foot & (lane_i == levels + row_i), 1.0, 0.0)
-    pick = pick + jnp.where(is_foot & (lane_i == levels + foot + row_i), float(lon_dev), 0.0)
-    pick = pick + jnp.where((row_i == foot) & (lane_i == levels + 2 * foot), 1.0, 0.0)
-    pick = pick.astype(BF16)
-    block = 512
+    chunk = 8
+    span = foot * chunk
+    row_i = lax.broadcasted_iota(I32, (LANES, LANES), 0) - levels
+    lane_i = lax.broadcasted_iota(I32, (LANES, LANES), 1)
+    pick = (row_i >= 0) & (row_i <= 2 * foot) & (row_i == lane_i // chunk)
+    pick = jnp.where(pick, 1.0, 0.0).astype(BF16)
+    block = 256
+    own = lax.broadcasted_iota(I32, (block, LANES), 0) % chunk
+    own = own == lax.broadcasted_iota(I32, (block, LANES), 1) % chunk
+    chunk_i = lax.broadcasted_iota(I32, (block // chunk, block), 0)
+    gather = chunk_i == lax.broadcasted_iota(I32, (block // chunk, block), 1) // chunk
+    gather = jnp.where(gather, 1.0, 0.0).astype(BF16)
+    is_cell = lax.broadcasted_iota(I32, (block // chunk, LANES), 1) < span
     for b in range(slots // block):
         rows = slice(b * block, (b + 1) * block)
         part = got_ref[rows, :]
-        meta = lax.dot_general(pick, part, (((1,), (1,)), ((), ())), preferred_element_type=F32)
-        meta_v[:, rows] = meta.astype(I32)
+        fields = jnp.dot(part, pick, preferred_element_type=F32)
+        fields = jnp.where(own, fields, 0.0).astype(BF16)
+        table = jnp.dot(gather, fields, preferred_element_type=F32)
+        turned = pltpu.roll(table, LANES - span, 1)
+        table = jnp.where(is_cell, table + turned * float(lon_dev), table)
+        at = b * (block // chunk)
+        fields_v[at : at + block // chunk, :] = table
         share_ref[rows, :] = part.astype(F32)
-    copy = pltpu.make_async_copy(meta_v, meta_s, sems.at[1])
-    copy.start()
+    lanes = list(range(span)) + [2 * span]
+    for i in range(slots // chunk // LANES):
+        cols = slice(i * LANES, (i + 1) * LANES)
+        turned = fields_v[cols, :].T.astype(I32)
+        for k, lane in enumerate(lanes):
+            meta_v[k, :, cols] = turned[lane : lane + 1, :]
+    copies = [pltpu.make_async_copy(meta_v.at[k, 0], t, sems.at[k + 1]) for k, t in enumerate(tables)]
+    for copy in copies:
+        copy.start()
     accs = (acc0, acc1, acc2, acc3)
     for acc in accs[1:]:
         acc[...] = jnp.zeros_like(acc)
     load.wait()
-    copy.wait()
-    chunk = 8
+    for copy in copies:
+        copy.wait()
+    per_source = capacity // chunk
 
     def one_source(s, _):
-        base = s * capacity
-        n_chunks = meta_s[foot, base]
-        for c in range(1, capacity // chunk):
-            n_chunks = n_chunks + meta_s[foot, base + c * chunk]
+        base = s * per_source
+        n_chunks = tables[span][base]
+        for c in range(1, per_source):
+            n_chunks = n_chunks + tables[span][base + c]
 
         def one_chunk(c, _):
-            first = base + c * chunk
+            first = pl.multiple_of(c * chunk, chunk)
             for u in range(chunk):
                 row = share_ref[pl.ds(first + u, 1), :]
                 for f in range(foot):
-                    cell = meta_s[f, first + u]
+                    cell = tables[f * chunk + u][c]
                     accs[f][pl.ds(cell, 1), :] = accs[f][pl.ds(cell, 1), :] + row
             return 0
 
-        lax.fori_loop(0, n_chunks, one_chunk, 0)
+        lax.fori_loop(base, base + n_chunks, one_chunk, 0)
         return 0
 
     lax.fori_loop(0, ndev, one_source, 0)
@@ -217,7 +236,7 @@
 def prepare_kernel(lat_dev, back_ref, vert_ref, out_ref, mix_ref):
     ncells, levels = back_ref.shape
     lon_dev = ncells // lat_dev
-    v_high, v_low = split(vert_ref[...])
+    v_high, v_low = split(vert_ref[...].T)
     mix_ref[...] = jnp.zeros_like(mix_ref)
     mix_ref[:levels, :levels] = v_high
     mix_ref[:levels, LANES : LANES + levels] = v_low
@@ -278,10 +297,9 @@
             quantise([y[:, k : k + LANES] for k in range(0, width, LANES)], out_ref, place)
 
 
-def unpack_kernel(got_ref, out_ref):
+def unpack_kernel(got_ref, out_ref, held_ref):
     lon_dev, lats, levels = out_ref.shape
     lane = lax.broadcasted_iota(I32, (lon_dev, LANES), 1)
-    flat = out_ref.reshape(lon_dev * lats, levels)
     for t in range(got_ref.shape[0]):
         x = dequantise(got_ref, t)
         o = [x[:, k * LANES : (k + 1) * LANES] for k in range(3)]
@@ -292,7 +310,10 @@
             pltpu.roll(o[2], 96, 1),
         ]
         for j in range(4):
-            flat[pl.ds(t * 4 + j, lon_dev, stride=lats), :] = a[j][:, :levels]
+            at = (t * 4 + j) * lon_dev
+            held_ref[at : at + lon_dev, :] = a[j]
+    for i in range(lon_dev):
+        out_ref[i] = held_ref[pl.ds(i, lats, stride=lon_dev), :][:, :levels]
 
 
 def per_device(
@@ -325,8 +346,8 @@
             pltpu.VMEM((nrows, LANES), F32),
             pltpu.VMEM((slots + 8, LANES), F32),
             pltpu.VMEM((slots + 8, LANES), F32),
-            pltpu.VMEM((nrows // LANES, LANES), I32),
-            pltpu.SMEM((nrows // LANES, LANES), I32),
+            pltpu.VMEM((1, nrows), I32),
+            pltpu.SMEM((nrows,), I32),
             pltpu.SemaphoreType.DMA,
         ],
         compiler_params=params(),
@@ -339,7 +360,7 @@
         valid_count.reshape(1, nrows),
         jacobian.T,
     )
-    sent, background, turned = lax.optimization_barrier((sent, background, vertical.T))
+    sent, background, vertical = lax.optimization_barrier((sent, background, vertical))
     got = lax.all_to_all(
         sent.reshape(ndev, capacity, LANES), ("lon", "lat"), split_axis=0, concat_axis=0, tiled=True
     ).reshape(slots, LANES)
@@ -354,7 +375,7 @@
         compiler_params=params(),
         cost_estimate=pl.CostEstimate(flops=0, bytes_accessed=12_000_000, transcendentals=0),
         name="prepare",
-    )(background.reshape(ncells, levels), turned)
+    )(background.reshape(ncells, levels), vertical)
     acc = pltpu.VMEM((ncells + 8, LANES), F32)
     field = pl.pallas_call(
         lambda *refs: spread_kernel(capacity, lon_dev, lat_dev, levels, *refs),
@@ -367,10 +388,11 @@
             acc,
             acc,
             acc,
-            pltpu.VMEM((8, slots), I32),
-            pltpu.SMEM((8, slots), I32),
-            pltpu.SemaphoreType.DMA((2,)),
-        ],
+            pltpu.VMEM((slots // 8, LANES), F32),
+            pltpu.VMEM((33, 1, slots // 8), I32),
+            pltpu.SemaphoreType.DMA((34,)),
+        ]
+        + [pltpu.SMEM((slots // 8,), I32)] * 33,
         compiler_params=params(),
         name="spread",
     )(got, ordered, mixer)
@@ -413,6 +435,7 @@
         out_shape=jax.ShapeDtypeStruct((lon_dev, lat_dev, levels), F32),
         in_specs=[pl.BlockSpec((2,) + coded[1:], lambda g: (g, 0, 0))],
         out_specs=pl.BlockSpec((lon_dev, 8, levels), lambda g: (0, g, 0)),
+        scratch_shapes=[pltpu.VMEM((8 * lon_dev, LANES), F32)],
         compiler_params=params(),
         name="unpack",
     )(back)

time: 142 us -> 137 us (0.965); the launches traced: 141 us -> 135 us
  starting transfers between devices: 30.9 us -> 27.2 us
  local copies, waits for them, and re-layouts: 5.23 us -> 3.73 us
    all_to_all x1, starting transfers between devices: 19.7 us -> 16.2 us  [per_device(): lax.all_to_all(field, 'lon', split_axis=0, concat_axis=0, tiled=True)]
    pallas_call x1, Pallas kernels: 8.32 us -> 5.12 us  [per_device(): pl.pallas_call(lambda *refs: dispatch_kernel(capacity, *refs), out_shape=...]
    unnamed x11 -> x10, local copies, waits for them, and re-layouts: 3.95 us -> 2.44 us
  transfers between devices with their start and end apart: 2 -> 2, of which waited for: 2 -> 2; matrix products, arithmetic and copies ran while one was open for 3% -> 3% of each run, Pallas kernels for 6% -> 7%
where the time goes in v3:
time: 137 us; the launch traced here: 135 us
  Pallas kernels  50.6 us (37%)
  starting transfers between devices  27.2 us (20%)
  waiting for transfers between devices  27.1 us (20%)
  blocking collectives  23.4 us (17%)
  local copies, waits for them, and re-layouts  3.73 us (3%)
  other arithmetic  2.1 us (2%)
    all_to_all x1, blocking collectives, per_device(): lax.all_to_all(result, 'lon', split_axis=0, concat_axis=0, tiled=True)  23.4 us
    pallas_call x1, Pallas kernels, per_device(): pl.pallas_call(lambda *refs: spread_kernel(capacity, lon_dev, lat_dev, le...  20.4 us
    all_to_all x1, starting transfers between devices, per_device(): lax.all_to_all(field, 'lon', split_axis=0, concat_axis=0, tiled=True)  16.2 us
    all_to_all x1, waiting for transfers between devices, per_device(): lax.all_to_all(sent.reshape(ndev, capacity, LANES), ('lon', 'lat'), split...  14.8 us
    all_to_all x1, waiting for transfers between devices, per_device(): lax.all_to_all(field, 'lon', split_axis=0, concat_axis=0, tiled=True)  12.3 us
    all_to_all x1, starting transfers between devices, per_device(): lax.all_to_all(sent.reshape(ndev, capacity, LANES), ('lon', 'lat'), split...  10.9 us
    pallas_call x1, Pallas kernels, per_device(): pl.pallas_call(conv_kernel, out_shape=jax.ShapeDtypeStruct(coded, I16), i...  8.98 us
    pallas_call x1, Pallas kernels, per_device(): pl.pallas_call(unpack_kernel, grid=(n_lon // 2,), out_shape=jax.ShapeDtyp...  7.05 us
  transfers between devices with their start and end apart: 2, of which 2 were waited for; matrix products, arithmetic and copies ran while one was open for 3% of the time, Pallas kernels for 7%

profile of v3, /device:TPU:4, one launch (start us, length us, event | category | flops | bytes accessed | tf_op | source)
XLA Modules:
  0.0 134.7 jit_solution(7367653968176053675)
XLA Ops:
  0.7 5.1 %dispatch.1 = bf16[5120,128]{1,0:T(8,128)(2,1)} custom-call(s32[1]{0:T(128)S(6)} %copy.10.refs_0_, bf16[2048,128]{1,0:T(8,128)(2,1)} %refs_1_.1, s32[1,2048]{1,0:T(1,128)} %bitcast.16, s32[4,2048]{1,0:T(4,128)} %bitcast.12, s32[1,2048]{1,0:T(1,128)} %bitcast.17, bf16[96,128]{1,0:T(8,128)(2,1)} %bitcast.14), custom_call_target="tpu_custom_call" | custom-call | tf_op jit(solution)/shard_map/dispatch/pallas_call | solution.py:340
  5.8 10.9 %all-to-all-start = ((bf16[128,40,128]{2,1,0:T(8,128)(2,1)}), bf16[128,40,128]{2,1,0:T(8,128)(2,1)S(1)}, u32[]{:S(2)}, u32[]{:S(2)}) async-start(bf16[128,40,128]{2,1,0:T(8,128)(2,1)} %bitcast.9), calls=%async_computation | async-start | bytes 2621440 | tf_op jit(solution)/shard_map/all_to_all | solution.py:364
  16.7 5.9 %prepare.1 = (f32[6144,128]{1,0:T(8,128)}, bf16[256,256]{1,0:T(8,128)(2,1)}) custom-call(f32[6144,96]{1,0:T(8,128)} %bitcast.11, f32[96,96]{1,0:T(8,128)} %refs_1_.2), custom_call_target="tpu_custom_call" | custom-call | bytes 12000000 | tf_op jit(solution)/shard_map/prepare/pallas_call | solution.py:367
  22.6 14.8 %all-to-all-done = bf16[128,40,128]{2,1,0:T(8,128)(2,1)S(1)} async-done(((bf16[128,40,128]{2,1,0:T(8,128)(2,1)}), bf16[128,40,128]{2,1,0:T(8,128)(2,1)S(1)}, u32[]{:S(2)}, u32[]{:S(2)}) %all-to-all-start) | async-done | bytes 1310752 | tf_op jit(solution)/shard_map/all_to_all | solution.py:364
  37.4 0.0 copy-start
  37.4 1.1 copy-done
  38.5 20.4 %spread.1 = s16[16,104,384]{2,1,0:T(8,128)(2,1)} custom-call(bf16[5120,128]{1,0:T(8,128)(2,1)} %bitcast.10, f32[6144,128]{1,0:T(8,128)} %get-tuple-element.17.refs_1_, bf16[256,256]{1,0:T(8,128)(2,1)} %get-tuple-element.18.refs_2_), custom_call_target="tpu_custom_call" | custom-call | tf_op jit(solution)/shard_map/spread/pallas_call | solution.py:380
  58.9 0.0 copy-start.2
  58.9 16.2 %all-to-all-start.1 = ((s16[16,104,384]{2,1,0:T(8,128)(2,1)}), s16[16,104,384]{2,1,0:T(8,128)(2,1)S(1)}, u32[]{:S(2)}, u32[]{:S(2)}) async-start(s16[16,104,384]{2,1,0:T(8,128)(2,1)} %spread.1), calls=%async_computation.1 | async-start | bytes 2555904 | tf_op jit(solution)/shard_map/all_to_all | solution.py:416
  75.1 0.0 copy-done.2
  75.1 0.5 slice.41
  75.7 0.1 slice.42
  75.8 0.1 fusion.1
  75.8 0.5 slice.49
  76.3 0.1 slice.50
  76.4 0.1 reverse.6
  76.5 0.1 slice.55
  76.6 0.1 slice.46
  76.7 0.7 fusion
  77.4 0.1 reverse.5
  77.5 0.1 slice.54
  77.5 0.7 pad_maximum_fusion.2
  78.3 0.6 pad_maximum_fusion.kern_ref
  78.9 3.1 %toeplitz.1 = (bf16[768,768]{1,0:T(8,128)(2,1)}, bf16[768,768]{1,0:T(8,128)(2,1)}, bf16[768,768]{1,0:T(8,128)(2,1)}, bf16[768,768]{1,0:T(8,128)(2,1)}) custom-call(f32[2,768]{1,0:T(2,128)} %pad_maximum_fusion.kern_ref), custom_call_target="tpu_custom_call" | custom-call | tf_op jit(solution)/shard_map/toeplitz/pallas_call | solution.py:407
  82.0 12.3 %all-to-all-done.1.got_ref = s16[16,104,384]{2,1,0:T(8,128)(2,1)S(1)} async-done(((s16[16,104,384]{2,1,0:T(8,128)(2,1)}), s16[16,104,384]{2,1,0:T(8,128)(2,1)S(1)}, u32[]{:S(2)}, u32[]{:S(2)}) %all-to-all-start.1) | async-done | bytes 1277984 | tf_op jit(solution)/shard_map/all_to_all | solution.py:416
  94.3 0.0 copy-start.1
  94.3 1.0 copy-done.1
  95.3 9.0 %convolve.1 = s16[16,104,384]{2,1,0:T(8,128)(2,1)} custom-call(s16[16,104,384]{2,1,0:T(8,128)(2,1)} %copy-done.1, bf16[768,768]{1,0:T(8,128)(2,1)} %get-tuple-element.19.refs_0_, bf16[768,768]{1,0:T(8,128)(2,1)} %get-tuple-element.20.refs_1_, bf16[768,768]{1,0:T(8,128)(2,1)} %get-tuple-element.21.refs_2_, bf16[768,768]{1,0:T(8,128)(2,1)} %get-tuple-element.22.refs_3_), custom_call_target="tpu_custom_call" | custom-call | tf_op jit(solution)/shard_map/convolve/pallas_call | solution.py:419
  104.3 23.4 %all_to_all.15.got_ref = s16[16,104,384]{2,1,0:T(8,128)(2,1)} all-to-all(s16[16,104,384]{2,1,0:T(8,128)(2,1)} %convolve.1), channel_id=1, replica_groups=mesh['lon'=16,'lat'=8] {'lon'}, dimensions={0} | all-to-all | bytes 2555904 | tf_op jit(solution)/shard_map/all_to_all | solution.py:431
  127.6 7.1 %unpack.1 = f32[96,64,96]{2,1,0:T(8,128)} custom-call(s16[16,104,384]{2,1,0:T(8,128)(2,1)} %all_to_all.15.got_ref), custom_call_target="tpu_custom_call" | custom-call | tf_op jit(solution)/shard_map/unpack/pallas_call | solution.py:432
  (2 shorter events, 0.0 us)
Async XLA Ops:
  5.8 31.6 %all-to-all-start = ((bf16[128,40,128]{2,1,0:T(8,128)(2,1)}), bf16[128,40,128]{2,1,0:T(8,128)(2,1)S(1)}, u32[]{:S(2)}, u32[]{:S(2)}) async-start(bf16[128,40,128]{2,1,0:T(8,128)(2,1)} %bitcast.9), calls=%async_computation | async-start | bytes 2621440 | tf_op jit(solution)/shard_map/all_to_all | solution.py:364
  37.4 1.1 copy-start
  58.9 16.2 %copy-start.2 = (f32[1536]{0:T(1024)S(1)}, f32[1536]{0:T(1024)}, u32[]{:S(2)}) copy-start(f32[1536]{0:T(1024)} %param.17) | copy-start | bytes 18436
  58.9 35.3 %all-to-all-start.1 = ((s16[16,104,384]{2,1,0:T(8,128)(2,1)}), s16[16,104,384]{2,1,0:T(8,128)(2,1)S(1)}, u32[]{:S(2)}, u32[]{:S(2)}) async-start(s16[16,104,384]{2,1,0:T(8,128)(2,1)} %spread.1), calls=%async_computation.1 | async-start | bytes 2555904 | tf_op jit(solution)/shard_map/all_to_all | solution.py:416
  94.3 1.0 copy-start.1

commit v4 on v3

--- a/solution.py
+++ b/solution.py
@@ -10,6 +10,7 @@
 I32 = jnp.int32
 I16 = jnp.int16
 LANES = 128
+N_ACC = 8
 TOP = 32700.0
 LOWEST = -110.0
 CODE_ROWS = 8
@@ -133,20 +134,17 @@
     mix_ref,
     out_ref,
     share_ref,
-    acc0,
-    acc1,
-    acc2,
-    acc3,
     fields_v,
     meta_v,
     sems,
-    *tables,
+    *held,
 ):
+    accs, tables = held[:N_ACC], held[N_ACC:]
     slots = got_ref.shape[0]
     ndev = slots // capacity
     ncells = lon_dev * lat_dev
     foot = 4
-    load = pltpu.make_async_copy(back_ref, acc0.at[pl.ds(0, ncells), :], sems.at[0])
+    load = pltpu.make_async_copy(back_ref, accs[0].at[pl.ds(0, ncells), :], sems.at[0])
     load.start()
     chunk = 8
     span = foot * chunk
@@ -171,7 +169,6 @@
         table = jnp.where(is_cell, table + turned * float(lon_dev), table)
         at = b * (block // chunk)
         fields_v[at : at + block // chunk, :] = table
-        share_ref[rows, :] = part.astype(F32)
     lanes = list(range(span)) + [2 * span]
     for i in range(slots // chunk // LANES):
         cols = slice(i * LANES, (i + 1) * LANES)
@@ -181,7 +178,7 @@
     copies = [pltpu.make_async_copy(meta_v.at[k, 0], t, sems.at[k + 1]) for k, t in enumerate(tables)]
     for copy in copies:
         copy.start()
-    accs = (acc0, acc1, acc2, acc3)
+    share_ref[...] = got_ref[...].astype(F32)
     for acc in accs[1:]:
         acc[...] = jnp.zeros_like(acc)
     load.wait()
@@ -201,7 +198,8 @@
                 row = share_ref[pl.ds(first + u, 1), :]
                 for f in range(foot):
                     cell = tables[f * chunk + u][c]
-                    accs[f][pl.ds(cell, 1), :] = accs[f][pl.ds(cell, 1), :] + row
+                    acc = accs[(u * foot + f) % N_ACC]
+                    acc[pl.ds(cell, 1), :] = acc[pl.ds(cell, 1), :] + row
             return 0
 
         lax.fori_loop(base, base + n_chunks, one_chunk, 0)
@@ -212,7 +210,10 @@
 
     def one_group(t, _):
         rows = pl.ds(pl.multiple_of(t * 4 * lon_dev, 4 * lon_dev), 4 * lon_dev)
-        total = (acc0[rows, :] + acc1[rows, :]) + (acc2[rows, :] + acc3[rows, :])
+        sums = [acc[rows, :] for acc in accs]
+        while len(sums) > 1:
+            sums = [a + b for a, b in zip(sums[::2], sums[1::2])]
+        total = sums[0]
         high, low = split(total)
         both = jnp.dot(
             jnp.concatenate([high, low], axis=1), mix_ref[...], preferred_element_type=F32
@@ -313,7 +314,62 @@
             at = (t * 4 + j) * lon_dev
             held_ref[at : at + lon_dev, :] = a[j]
     for i in range(lon_dev):
-        out_ref[i] = held_ref[pl.ds(i, lats, stride=lon_dev), :][:, :levels]
+        for g in range(0, lats, 8):
+            picked = held_ref[pl.ds(g * lon_dev + i, 8, stride=lon_dev), :]
+            out_ref[i, g : g + 8, :] = picked[:, :levels]
+
+
+def call_spread(got, ordered, mixer, capacity, lon_dev, lat_dev, levels, coded):
+    slots = got.shape[0]
+    ncells = lon_dev * lat_dev
+    acc = pltpu.VMEM((ncells + 8, LANES), F32)
+    return pl.pallas_call(
+        lambda *refs: spread_kernel(capacity, lon_dev, lat_dev, levels, *refs),
+        out_shape=jax.ShapeDtypeStruct(coded, I16),
+        in_specs=[vmem(1)[0], pl.BlockSpec(memory_space=pl.ANY), vmem(1)[0]],
+        out_specs=vmem(1)[0],
+        scratch_shapes=[
+            pltpu.VMEM((slots, LANES), F32),
+            pltpu.VMEM((slots // 8, LANES), F32),
+            pltpu.VMEM((33, 1, slots // 8), I32),
+            pltpu.SemaphoreType.DMA((34,)),
+        ]
+        + [acc] * N_ACC
+        + [pltpu.SMEM((slots // 8,), I32)] * 33,
+        compiler_params=params(),
+        name="spread",
+    )(got, ordered, mixer)
+
+
+def call_convolve(columns, toeplitz, half, width, coded):
+    part = pltpu.VMEM((half, width), BF16)
+    wide = pltpu.VMEM((half, width), F32)
+    return pl.pallas_call(
+        conv_kernel,
+        out_shape=jax.ShapeDtypeStruct(coded, I16),
+        in_specs=vmem(1) + [pl.BlockSpec(memory_space=pl.ANY)] * 4,
+        out_specs=vmem(1)[0],
+        scratch_shapes=[pltpu.VMEM((half, half), BF16)] * 4
+        + [part] * 4
+        + [wide] * 2
+        + [pltpu.SemaphoreType.DMA((4,))],
+        compiler_params=params(),
+        name="convolve",
+    )(columns, *toeplitz)
+
+
+def call_unpack(back, lon_dev, lat_dev, levels, coded):
+    n_lon = coded[0]
+    return pl.pallas_call(
+        unpack_kernel,
+        grid=(n_lon // 4,),
+        out_shape=jax.ShapeDtypeStruct((lon_dev, lat_dev, levels), F32),
+        in_specs=[pl.BlockSpec((4,) + coded[1:], lambda g: (g, 0, 0))],
+        out_specs=pl.BlockSpec((lon_dev, 16, levels), lambda g: (0, g, 0)),
+        scratch_shapes=[pltpu.VMEM((16 * lon_dev, LANES), F32)],
+        compiler_params=params(),
+        name="unpack",
+    )(back)
 
 
 def per_device(
@@ -376,26 +432,7 @@
         cost_estimate=pl.CostEstimate(flops=0, bytes_accessed=12_000_000, transcendentals=0),
         name="prepare",
     )(background.reshape(ncells, levels), vertical)
-    acc = pltpu.VMEM((ncells + 8, LANES), F32)
-    field = pl.pallas_call(
-        lambda *refs: spread_kernel(capacity, lon_dev, lat_dev, levels, *refs),
-        out_shape=jax.ShapeDtypeStruct(coded, I16),
-        in_specs=[vmem(1)[0], pl.BlockSpec(memory_space=pl.ANY), vmem(1)[0]],
-        out_specs=vmem(1)[0],
-        scratch_shapes=[
-            pltpu.VMEM((slots, LANES), F32),
-            acc,
-            acc,
-            acc,
-            acc,
-            pltpu.VMEM((slots // 8, LANES), F32),
-            pltpu.VMEM((33, 1, slots // 8), I32),
-            pltpu.SemaphoreType.DMA((34,)),
-        ]
-        + [pltpu.SMEM((slots // 8,), I32)] * 33,
-        compiler_params=params(),
-        name="spread",
-    )(got, ordered, mixer)
+    field = call_spread(got, ordered, mixer, capacity, lon_dev, lat_dev, levels, coded)
 
     half = n_lon * lon_dev // 2
     turned_kernel = jnp.roll(lon_kernel[::-1], 1)
@@ -414,31 +451,9 @@
     )(jnp.stack([plus, minus]))
 
     columns = lax.all_to_all(field, "lon", split_axis=0, concat_axis=0, tiled=True)
-    part = pltpu.VMEM((half, width), BF16)
-    wide = pltpu.VMEM((half, width), F32)
-    result = pl.pallas_call(
-        conv_kernel,
-        out_shape=jax.ShapeDtypeStruct(coded, I16),
-        in_specs=vmem(1) + [pl.BlockSpec(memory_space=pl.ANY)] * 4,
-        out_specs=vmem(1)[0],
-        scratch_shapes=[pltpu.VMEM((half, half), BF16)] * 4
-        + [part] * 4
-        + [wide] * 2
-        + [pltpu.SemaphoreType.DMA((4,))],
-        compiler_params=params(),
-        name="convolve",
-    )(columns, *toeplitz)
+    result = call_convolve(columns, toeplitz, half, width, coded)
     back = lax.all_to_all(result, "lon", split_axis=0, concat_axis=0, tiled=True)
-    return pl.pallas_call(
-        unpack_kernel,
-        grid=(n_lon // 2,),
-        out_shape=jax.ShapeDtypeStruct((lon_dev, lat_dev, levels), F32),
-        in_specs=[pl.BlockSpec((2,) + coded[1:], lambda g: (g, 0, 0))],
-        out_specs=pl.BlockSpec((lon_dev, 8, levels), lambda g: (0, g, 0)),
-        scratch_shapes=[pltpu.VMEM((8 * lon_dev, LANES), F32)],
-        compiler_params=params(),
-        name="unpack",
-    )(back)
+    return call_unpack(back, lon_dev, lat_dev, levels, coded)
 
 
 def solution(mesh):

time: 137 us -> 130 us (0.949)
  starting transfers between devices: 27.2 us -> 20.8 us
    all_to_all x1, starting transfers between devices: 16.2 us -> 9.73 us  [per_device(): lax.all_to_all(field, 'lon', split_axis=0, concat_axis=0, tiled=True)]
where the time goes in v4:
time: 130 us; the launch traced here: 128 us
  Pallas kernels  49.7 us (38%)
  waiting for transfers between devices  27.1 us (21%)
  blocking collectives  23.4 us (18%)
  starting transfers between devices  20.8 us (16%)
  local copies, waits for them, and re-layouts  3.73 us (3%)
  other arithmetic  2.1 us (2%)
    all_to_all x1, blocking collectives, per_device(): lax.all_to_all(result, 'lon', split_axis=0, concat_axis=0, tiled=True)  23.4 us
    pallas_call x1, Pallas kernels, call_spread(): pl.pallas_call(lambda *refs: spread_kernel(capacity, lon_dev, lat_dev, le...  21.5 us
    all_to_all x1, waiting for transfers between devices, per_device(): lax.all_to_all(sent.reshape(ndev, capacity, LANES), ('lon', 'lat'), split...  14.8 us
    all_to_all x1, waiting for transfers between devices, per_device(): lax.all_to_all(field, 'lon', split_axis=0, concat_axis=0, tiled=True)  12.3 us
    all_to_all x1, starting transfers between devices, per_device(): lax.all_to_all(sent.reshape(ndev, capacity, LANES), ('lon', 'lat'), split...  11.1 us
    all_to_all x1, starting transfers between devices, per_device(): lax.all_to_all(field, 'lon', split_axis=0, concat_axis=0, tiled=True)  9.73 us
    pallas_call x1, Pallas kernels, call_convolve(): pl.pallas_call(conv_kernel, out_shape=jax.ShapeDtypeStruct(coded, I16), i...  8.98 us
    pallas_call x1, Pallas kernels, per_device(): pl.pallas_call(lambda *refs: prepare_kernel(lat_dev, *refs), out_shape=(j...  5.93 us
  transfers between devices with their start and end apart: 2, of which 2 were waited for; matrix products, arithmetic and copies ran while one was open for 3% of the time, Pallas kernels for 7%

profile of v4, /device:TPU:4, one launch (start us, length us, event | category | flops | bytes accessed | tf_op | source)
XLA Modules:
  0.0 127.5 jit_solution(10354965865248168725)
XLA Ops:
  0.7 4.9 %dispatch.1 = bf16[5120,128]{1,0:T(8,128)(2,1)} custom-call(s32[1]{0:T(128)S(6)} %copy.10.refs_0_, bf16[2048,128]{1,0:T(8,128)(2,1)} %refs_1_.1, s32[1,2048]{1,0:T(1,128)} %bitcast.16, s32[4,2048]{1,0:T(4,128)} %bitcast.12, s32[1,2048]{1,0:T(1,128)} %bitcast.17, bf16[96,128]{1,0:T(8,128)(2,1)} %bitcast.14), custom_call_target="tpu_custom_call" | custom-call | tf_op jit(solution)/shard_map/dispatch/pallas_call | solution.py:396
  5.5 11.1 %all-to-all-start = ((bf16[128,40,128]{2,1,0:T(8,128)(2,1)}), bf16[128,40,128]{2,1,0:T(8,128)(2,1)S(1)}, u32[]{:S(2)}, u32[]{:S(2)}) async-start(bf16[128,40,128]{2,1,0:T(8,128)(2,1)} %bitcast.9), calls=%async_computation | async-start | bytes 2621440 | tf_op jit(solution)/shard_map/all_to_all | solution.py:420
  16.7 5.9 %prepare.1 = (f32[6144,128]{1,0:T(8,128)}, bf16[256,256]{1,0:T(8,128)(2,1)}) custom-call(f32[6144,96]{1,0:T(8,128)} %bitcast.11, f32[96,96]{1,0:T(8,128)} %refs_1_.2), custom_call_target="tpu_custom_call" | custom-call | bytes 12000000 | tf_op jit(solution)/shard_map/prepare/pallas_call | solution.py:423
  22.6 14.8 %all-to-all-done = bf16[128,40,128]{2,1,0:T(8,128)(2,1)S(1)} async-done(((bf16[128,40,128]{2,1,0:T(8,128)(2,1)}), bf16[128,40,128]{2,1,0:T(8,128)(2,1)S(1)}, u32[]{:S(2)}, u32[]{:S(2)}) %all-to-all-start) | async-done | bytes 1310752 | tf_op jit(solution)/shard_map/all_to_all | solution.py:420
  37.3 0.0 copy-start
  37.4 1.1 copy-done
  38.4 21.5 %spread.1 = s16[16,104,384]{2,1,0:T(8,128)(2,1)} custom-call(bf16[5120,128]{1,0:T(8,128)(2,1)} %bitcast.10, f32[6144,128]{1,0:T(8,128)} %get-tuple-element.17.refs_1_, bf16[256,256]{1,0:T(8,128)(2,1)} %get-tuple-element.18.refs_2_), custom_call_target="tpu_custom_call" | custom-call | tf_op jit(solution)/shard_map/spread/pallas_call | solution.py:326
  59.9 0.0 copy-start.2
  59.9 9.7 %all-to-all-start.1 = ((s16[16,104,384]{2,1,0:T(8,128)(2,1)}), s16[16,104,384]{2,1,0:T(8,128)(2,1)S(1)}, u32[]{:S(2)}, u32[]{:S(2)}) async-start(s16[16,104,384]{2,1,0:T(8,128)(2,1)} %spread.1), calls=%async_computation.1 | async-start | bytes 2555904 | tf_op jit(solution)/shard_map/all_to_all | solution.py:453
  69.7 0.0 copy-done.2
  69.7 0.5 slice.41
  70.2 0.1 slice.42
  70.3 0.1 fusion.1
  70.3 0.5 slice.49
  70.9 0.1 slice.50
  70.9 0.1 reverse.6
  71.0 0.1 slice.55
  71.1 0.1 slice.46
  71.2 0.7 fusion
  71.9 0.1 reverse.5
  72.0 0.1 slice.54
  72.0 0.7 pad_maximum_fusion.2
  72.8 0.6 pad_maximum_fusion.kern_ref
  73.4 3.1 %toeplitz.1 = (bf16[768,768]{1,0:T(8,128)(2,1)}, bf16[768,768]{1,0:T(8,128)(2,1)}, bf16[768,768]{1,0:T(8,128)(2,1)}, bf16[768,768]{1,0:T(8,128)(2,1)}) custom-call(f32[2,768]{1,0:T(2,128)} %pad_maximum_fusion.kern_ref), custom_call_target="tpu_custom_call" | custom-call | tf_op jit(solution)/shard_map/toeplitz/pallas_call | solution.py:444
  76.5 12.3 %all-to-all-done.1.got_ref = s16[16,104,384]{2,1,0:T(8,128)(2,1)S(1)} async-done(((s16[16,104,384]{2,1,0:T(8,128)(2,1)}), s16[16,104,384]{2,1,0:T(8,128)(2,1)S(1)}, u32[]{:S(2)}, u32[]{:S(2)}) %all-to-all-start.1) | async-done | bytes 1277984 | tf_op jit(solution)/shard_map/all_to_all | solution.py:453
  88.8 0.0 copy-start.1
  88.8 1.0 copy-done.1
  89.8 9.0 %convolve.1 = s16[16,104,384]{2,1,0:T(8,128)(2,1)} custom-call(s16[16,104,384]{2,1,0:T(8,128)(2,1)} %copy-done.1, bf16[768,768]{1,0:T(8,128)(2,1)} %get-tuple-element.19.refs_0_, bf16[768,768]{1,0:T(8,128)(2,1)} %get-tuple-element.20.refs_1_, bf16[768,768]{1,0:T(8,128)(2,1)} %get-tuple-element.21.refs_2_, bf16[768,768]{1,0:T(8,128)(2,1)} %get-tuple-element.22.refs_3_), custom_call_target="tpu_custom_call" | custom-call | tf_op jit(solution)/shard_map/convolve/pallas_call | solution.py:347
  98.8 23.4 %all_to_all.15.got_ref = s16[16,104,384]{2,1,0:T(8,128)(2,1)} all-to-all(s16[16,104,384]{2,1,0:T(8,128)(2,1)} %convolve.1), channel_id=1, replica_groups=mesh['lon'=16,'lat'=8] {'lon'}, dimensions={0} | all-to-all | bytes 2555904 | tf_op jit(solution)/shard_map/all_to_all | solution.py:455
  122.2 5.3 %unpack.1 = f32[96,64,96]{2,1,0:T(8,128)} custom-call(s16[16,104,384]{2,1,0:T(8,128)(2,1)} %all_to_all.15.got_ref), custom_call_target="tpu_custom_call" | custom-call | tf_op jit(solution)/shard_map/unpack/pallas_call | solution.py:363
  (2 shorter events, 0.0 us)
Async XLA Ops:
  5.5 31.8 %all-to-all-start = ((bf16[128,40,128]{2,1,0:T(8,128)(2,1)}), bf16[128,40,128]{2,1,0:T(8,128)(2,1)S(1)}, u32[]{:S(2)}, u32[]{:S(2)}) async-start(bf16[128,40,128]{2,1,0:T(8,128)(2,1)} %bitcast.9), calls=%async_computation | async-start | bytes 2621440 | tf_op jit(solution)/shard_map/all_to_all | solution.py:420
  37.3 1.1 copy-start
  59.9 9.8 %copy-start.2 = (f32[1536]{0:T(1024)S(1)}, f32[1536]{0:T(1024)}, u32[]{:S(2)}) copy-start(f32[1536]{0:T(1024)} %param.17) | copy-start | bytes 18436
  59.9 28.9 %all-to-all-start.1 = ((s16[16,104,384]{2,1,0:T(8,128)(2,1)}), s16[16,104,384]{2,1,0:T(8,128)(2,1)S(1)}, u32[]{:S(2)}, u32[]{:S(2)}) async-start(s16[16,104,384]{2,1,0:T(8,128)(2,1)} %spread.1), calls=%async_computation.1 | async-start | bytes 2555904 | tf_op jit(solution)/shard_map/all_to_all | solution.py:453
  88.8 1.0 copy-start.1

commit v5 on v4

--- a/solution.py
+++ b/solution.py
@@ -20,8 +20,8 @@
     return [pl.BlockSpec(memory_space=pltpu.VMEM)] * n
 
 
-def params():
-    return pltpu.CompilerParams(vmem_limit_bytes=56 * 1024 * 1024)
+def params(mib=56):
+    return pltpu.CompilerParams(vmem_limit_bytes=mib * 1024 * 1024)
 
 
 def quantise(tiles, out_ref, place):
@@ -129,14 +129,18 @@
     lon_dev,
     lat_dev,
     levels,
-    got_ref,
+    got_hbm,
     back_ref,
     mix_ref,
+    out_hbm,
+    got_ref,
     out_ref,
     share_ref,
     fields_v,
     meta_v,
     sems,
+    got_sems,
+    out_sems,
     *held,
 ):
     accs, tables = held[:N_ACC], held[N_ACC:]
@@ -146,6 +150,16 @@
     foot = 4
     load = pltpu.make_async_copy(back_ref, accs[0].at[pl.ds(0, ncells), :], sems.at[0])
     load.start()
+    n_gets = 4
+    piece = slots // n_gets
+    gets = []
+    for i in range(n_gets):
+        at = pl.ds(i * piece, piece)
+        get = pltpu.make_async_copy(got_hbm.at[at, :], got_ref.at[at, :], got_sems.at[i])
+        get.start()
+        gets.append(get)
+    for acc in accs[1:]:
+        acc[...] = jnp.zeros_like(acc)
     chunk = 8
     span = foot * chunk
     row_i = lax.broadcasted_iota(I32, (LANES, LANES), 0) - levels
@@ -160,6 +174,8 @@
     gather = jnp.where(gather, 1.0, 0.0).astype(BF16)
     is_cell = lax.broadcasted_iota(I32, (block // chunk, LANES), 1) < span
     for b in range(slots // block):
+        if b * block % piece == 0:
+            gets[b * block // piece].wait()
         rows = slice(b * block, (b + 1) * block)
         part = got_ref[rows, :]
         fields = jnp.dot(part, pick, preferred_element_type=F32)
@@ -179,8 +195,6 @@
     for copy in copies:
         copy.start()
     share_ref[...] = got_ref[...].astype(F32)
-    for acc in accs[1:]:
-        acc[...] = jnp.zeros_like(acc)
     load.wait()
     for copy in copies:
         copy.wait()
@@ -208,8 +222,9 @@
     lax.fori_loop(0, ndev, one_source, 0)
     lane = lax.broadcasted_iota(I32, (lon_dev, LANES), 1)
 
-    def one_group(t, _):
-        rows = pl.ds(pl.multiple_of(t * 4 * lon_dev, 4 * lon_dev), 4 * lon_dev)
+    puts = []
+    for t in range(ncells // (4 * lon_dev)):
+        rows = pl.ds(t * 4 * lon_dev, 4 * lon_dev)
         sums = [acc[rows, :] for acc in accs]
         while len(sums) > 1:
             sums = [a + b for a, b in zip(sums[::2], sums[1::2])]
@@ -229,9 +244,11 @@
             jnp.where(lane < 32, r2, r3),
         ]
         quantise(tiles, out_ref, t)
-        return 0
-
-    lax.fori_loop(0, ncells // (4 * lon_dev), one_group, 0, unroll=4)
+        put = pltpu.make_async_copy(out_ref.at[t], out_hbm.at[t], out_sems.at[t])
+        put.start()
+        puts.append(put)
+    for put in puts:
+        put.wait()
 
 
 def prepare_kernel(lat_dev, back_ref, vert_ref, out_ref, mix_ref):
@@ -267,35 +284,52 @@
             low_ref[i * block : (i + 1) * block, :] = low
 
 
-def conv_kernel(got_ref, *refs):
-    hbm, out_ref, held, (xph, xpl, xmh, xml, yp, ym, sems) = refs[:4], refs[4], refs[5:9], refs[9:]
-    loads = [pltpu.make_async_copy(a, b, sems.at[i]) for i, (a, b) in enumerate(zip(hbm, held))]
+def conv_kernel(*refs):
+    got_hbm, mats, out_hbm = refs[0], refs[1:5], refs[5]
+    got_ref, held, (xp, xm, yp, ym, out_ref, in_sems, mat_sems, out_sems) = (
+        refs[6],
+        refs[7:11],
+        refs[11:],
+    )
+    n_lon = got_ref.shape[0]
+    rows = got_ref.shape[1] - CODE_ROWS
+    width = got_ref.shape[2]
+    half = n_lon // 2
+    gets = [
+        pltpu.make_async_copy(got_hbm.at[s], got_ref.at[s], in_sems.at[s]) for s in range(n_lon)
+    ]
+    for s in range(half):
+        gets[s].start()
+        gets[s + half].start()
+    loads = [pltpu.make_async_copy(a, b, mat_sems.at[i]) for i, (a, b) in enumerate(zip(mats, held))]
     for load in loads:
         load.start()
     ph_ref, pl_ref, mh_ref, ml_ref = held
-    n_lon = got_ref.shape[0]
-    rows = got_ref.shape[1] - CODE_ROWS
-    half = n_lon // 2
     for s in range(half):
+        gets[s].wait()
+        gets[s + half].wait()
         a = dequantise(got_ref, s)
         b = dequantise(got_ref, s + half)
         at = slice(s * rows, (s + 1) * rows)
-        xph[at, :], xpl[at, :] = split(a + b)
-        xmh[at, :], xml[at, :] = split(a - b)
-    for load in loads:
-        load.wait()
-    for th, tl, xh, xl, y in ((ph_ref, pl_ref, xph, xpl, yp), (mh_ref, ml_ref, xmh, xml, ym)):
-        y[...] = (
-            jnp.dot(th[...], xh[...], preferred_element_type=F32)
-            + jnp.dot(tl[...], xh[...], preferred_element_type=F32)
-            + jnp.dot(th[...], xl[...], preferred_element_type=F32)
-        )
-    width = got_ref.shape[2]
+        xp[at, :width], xp[at, width:] = split(a + b)
+        xm[at, :width], xm[at, width:] = split(a - b)
+    for i, (th, tl, x, y) in enumerate(((ph_ref, pl_ref, xp, yp), (mh_ref, ml_ref, xm, ym))):
+        loads[2 * i].wait()
+        loads[2 * i + 1].wait()
+        both = jnp.dot(th[...], x[...], preferred_element_type=F32)
+        rest = jnp.dot(tl[...], x[:, :width], preferred_element_type=F32)
+        y[...] = both[:, :width] + (both[:, width:] + rest)
+    puts = []
     for s in range(half):
         at = slice(s * rows, (s + 1) * rows)
         plus, minus = yp[at, :], ym[at, :]
         for place, y in ((s, 0.5 * (plus + minus)), (s + half, 0.5 * (plus - minus))):
             quantise([y[:, k : k + LANES] for k in range(0, width, LANES)], out_ref, place)
+            put = pltpu.make_async_copy(out_ref.at[place], out_hbm.at[place], out_sems.at[place])
+            put.start()
+            puts.append(put)
+    for put in puts:
+        put.wait()
 
 
 def unpack_kernel(got_ref, out_ref, held_ref):
@@ -326,13 +360,17 @@
     return pl.pallas_call(
         lambda *refs: spread_kernel(capacity, lon_dev, lat_dev, levels, *refs),
         out_shape=jax.ShapeDtypeStruct(coded, I16),
-        in_specs=[vmem(1)[0], pl.BlockSpec(memory_space=pl.ANY), vmem(1)[0]],
-        out_specs=vmem(1)[0],
+        in_specs=[pl.BlockSpec(memory_space=pl.ANY)] * 2 + vmem(1),
+        out_specs=pl.BlockSpec(memory_space=pl.ANY),
         scratch_shapes=[
+            pltpu.VMEM((slots, LANES), BF16),
+            pltpu.VMEM(coded, I16),
             pltpu.VMEM((slots, LANES), F32),
             pltpu.VMEM((slots // 8, LANES), F32),
             pltpu.VMEM((33, 1, slots // 8), I32),
             pltpu.SemaphoreType.DMA((34,)),
+            pltpu.SemaphoreType.DMA((4,)),
+            pltpu.SemaphoreType.DMA((coded[0],)),
         ]
         + [acc] * N_ACC
         + [pltpu.SMEM((slots // 8,), I32)] * 33,
@@ -342,17 +380,25 @@
 
 
 def call_convolve(columns, toeplitz, half, width, coded):
-    part = pltpu.VMEM((half, width), BF16)
+    part = pltpu.VMEM((half, 2 * width), BF16)
     wide = pltpu.VMEM((half, width), F32)
+    n_lon = coded[0]
+    anywhere = pl.BlockSpec(memory_space=pl.ANY)
     return pl.pallas_call(
         conv_kernel,
         out_shape=jax.ShapeDtypeStruct(coded, I16),
-        in_specs=vmem(1) + [pl.BlockSpec(memory_space=pl.ANY)] * 4,
-        out_specs=vmem(1)[0],
-        scratch_shapes=[pltpu.VMEM((half, half), BF16)] * 4
-        + [part] * 4
+        in_specs=[anywhere] * 5,
+        out_specs=anywhere,
+        scratch_shapes=[pltpu.VMEM(coded, I16)]
+        + [pltpu.VMEM((half, half), BF16)] * 4
+        + [part] * 2
         + [wide] * 2
-        + [pltpu.SemaphoreType.DMA((4,))],
+        + [
+            pltpu.VMEM(coded, I16),
+            pltpu.SemaphoreType.DMA((n_lon,)),
+            pltpu.SemaphoreType.DMA((4,)),
+            pltpu.SemaphoreType.DMA((n_lon,)),
+        ],
         compiler_params=params(),
         name="convolve",
     )(columns, *toeplitz)
@@ -428,7 +474,7 @@
         ),
         in_specs=vmem(2),
         out_specs=tuple(vmem(2)),
-        compiler_params=params(),
+        compiler_params=params(63),
         cost_estimate=pl.CostEstimate(flops=0, bytes_accessed=12_000_000, transcendentals=0),
         name="prepare",
     )(background.reshape(ncells, levels), vertical)
@@ -446,7 +492,7 @@
         out_shape=(square,) * 4,
         in_specs=vmem(1),
         out_specs=tuple(vmem(4)),
-        compiler_params=params(),
+        compiler_params=params(63),
         name="toeplitz",
     )(jnp.stack([plus, minus]))
 

time: 130 us -> 124 us (0.954)
  starting transfers between devices: 20.8 us -> 16.8 us
  local copies, waits for them, and re-layouts: 3.73 us -> 1.67 us
    all_to_all x1, starting transfers between devices: 9.73 us -> 5.91 us  [per_device(): lax.all_to_all(field, 'lon', split_axis=0, concat_axis=0, tiled=True)]
    unnamed x10 -> x6, local copies, waits for them, and re-layouts: 2.44 us -> 0.33 us
where the time goes in v5:
time: 124 us; the launch traced here: 122 us
  Pallas kernels  50.6 us (41%)
  waiting for transfers between devices  26.7 us (22%)
  blocking collectives  23.4 us (19%)
  starting transfers between devices  16.8 us (14%)
  other arithmetic  2.16 us (2%)
  local copies, waits for them, and re-layouts  1.67 us (1%)
    all_to_all x1, blocking collectives, per_device(): lax.all_to_all(result, 'lon', split_axis=0, concat_axis=0, tiled=True)  23.4 us
    pallas_call x1, Pallas kernels, call_spread(): pl.pallas_call(lambda *refs: spread_kernel(capacity, lon_dev, lat_dev, le...  22.7 us
    all_to_all x1, waiting for transfers between devices, per_device(): lax.all_to_all(sent.reshape(ndev, capacity, LANES), ('lon', 'lat'), split...  14.5 us
    all_to_all x1, waiting for transfers between devices, per_device(): lax.all_to_all(field, 'lon', split_axis=0, concat_axis=0, tiled=True)  12.2 us
    all_to_all x1, starting transfers between devices, per_device(): lax.all_to_all(sent.reshape(ndev, capacity, LANES), ('lon', 'lat'), split...  10.9 us
    pallas_call x1, Pallas kernels, call_convolve(): pl.pallas_call(conv_kernel, out_shape=jax.ShapeDtypeStruct(coded, I16), i...  7.8 us
    pallas_call x1, Pallas kernels, per_device(): pl.pallas_call(lambda *refs: prepare_kernel(lat_dev, *refs), out_shape=(j...  5.93 us
    all_to_all x1, starting transfers between devices, per_device(): lax.all_to_all(field, 'lon', split_axis=0, concat_axis=0, tiled=True)  5.91 us
  transfers between devices with their start and end apart: 2, of which 2 were waited for; matrix products, arithmetic and copies ran while one was open for 3% of the time, Pallas kernels for 7%

profile of v5, /device:TPU:4, one launch (start us, length us, event | category | flops | bytes accessed | tf_op | source)
XLA Modules:
  0.0 122.0 jit_solution(6701067242577300365)
XLA Ops:
  0.7 5.7 %dispatch.1 = bf16[5120,128]{1,0:T(8,128)(2,1)} custom-call(s32[1]{0:T(128)S(6)} %copy.10.refs_0_, bf16[2048,128]{1,0:T(8,128)(2,1)} %refs_1_.1, s32[1,2048]{1,0:T(1,128)} %bitcast.15, s32[4,2048]{1,0:T(4,128)} %bitcast.11, s32[1,2048]{1,0:T(1,128)} %bitcast.16, bf16[96,128]{1,0:T(8,128)(2,1)} %bitcast.13), custom_call_target="tpu_custom_call" | custom-call | tf_op jit(solution)/shard_map/dispatch/pallas_call | solution.py:442
  6.4 10.9 %all-to-all-start = ((bf16[128,40,128]{2,1,0:T(8,128)(2,1)}), bf16[128,40,128]{2,1,0:T(8,128)(2,1)}, u32[]{:S(2)}, u32[]{:S(2)}) async-start(bf16[128,40,128]{2,1,0:T(8,128)(2,1)} %bitcast.9), calls=%async_computation | async-start | bytes 2621440 | tf_op jit(solution)/shard_map/all_to_all | solution.py:466
  17.3 5.9 %prepare.1 = (f32[6144,128]{1,0:T(8,128)}, bf16[256,256]{1,0:T(8,128)(2,1)}) custom-call(f32[6144,96]{1,0:T(8,128)} %bitcast.10, f32[96,96]{1,0:T(8,128)} %refs_1_.2), custom_call_target="tpu_custom_call" | custom-call | bytes 12000000 | tf_op jit(solution)/shard_map/prepare/pallas_call | solution.py:469
  23.2 14.5 %all-to-all-done = bf16[128,40,128]{2,1,0:T(8,128)(2,1)} async-done(((bf16[128,40,128]{2,1,0:T(8,128)(2,1)}), bf16[128,40,128]{2,1,0:T(8,128)(2,1)}, u32[]{:S(2)}, u32[]{:S(2)}) %all-to-all-start) | async-done | bytes 1310752 | tf_op jit(solution)/shard_map/all_to_all | solution.py:466
  37.7 22.7 %spread.1 = s16[16,104,384]{2,1,0:T(8,128)(2,1)} custom-call(bf16[5120,128]{1,0:T(8,128)(2,1)} %bitcast.5.refs_0_, f32[6144,128]{1,0:T(8,128)} %get-tuple-element.17.refs_1_, bf16[256,256]{1,0:T(8,128)(2,1)} %get-tuple-element.18.refs_2_), custom_call_target="tpu_custom_call" | custom-call | tf_op jit(solution)/shard_map/spread/pallas_call | solution.py:360
  60.4 0.0 copy-start
  60.4 5.9 %all-to-all-start.1 = ((s16[16,104,384]{2,1,0:T(8,128)(2,1)}), s16[16,104,384]{2,1,0:T(8,128)(2,1)}, u32[]{:S(2)}, u32[]{:S(2)}) async-start(s16[16,104,384]{2,1,0:T(8,128)(2,1)} %spread.1), calls=%async_computation.1 | async-start | bytes 2555904 | tf_op jit(solution)/shard_map/all_to_all | solution.py:499
  66.3 0.0 copy-done
  66.3 0.6 slice.41
  66.9 0.1 slice.42
  67.0 0.1 fusion.1
  67.0 0.5 slice.49
  67.5 0.1 slice.50
  67.6 0.1 reverse.6
  67.7 0.1 slice.55
  67.8 0.1 slice.46
  67.9 0.8 fusion
  68.6 0.1 reverse.5
  68.7 0.1 slice.54
  68.8 0.7 pad_maximum_fusion.2
  69.5 0.6 pad_maximum_fusion.kern_ref
  70.1 3.1 %toeplitz.1 = (bf16[768,768]{1,0:T(8,128)(2,1)}, bf16[768,768]{1,0:T(8,128)(2,1)}, bf16[768,768]{1,0:T(8,128)(2,1)}, bf16[768,768]{1,0:T(8,128)(2,1)}) custom-call(f32[2,768]{1,0:T(2,128)} %pad_maximum_fusion.kern_ref), custom_call_target="tpu_custom_call" | custom-call | tf_op jit(solution)/shard_map/toeplitz/pallas_call | solution.py:490
  73.2 12.2 %all-to-all-done.1.refs_0_ = s16[16,104,384]{2,1,0:T(8,128)(2,1)} async-done(((s16[16,104,384]{2,1,0:T(8,128)(2,1)}), s16[16,104,384]{2,1,0:T(8,128)(2,1)}, u32[]{:S(2)}, u32[]{:S(2)}) %all-to-all-start.1) | async-done | bytes 1277984 | tf_op jit(solution)/shard_map/all_to_all | solution.py:499
  85.4 7.8 %convolve.1 = s16[16,104,384]{2,1,0:T(8,128)(2,1)} custom-call(s16[16,104,384]{2,1,0:T(8,128)(2,1)} %all-to-all-done.1.refs_0_, bf16[768,768]{1,0:T(8,128)(2,1)} %get-tuple-element.19.refs_1_, bf16[768,768]{1,0:T(8,128)(2,1)} %get-tuple-element.20.refs_2_, bf16[768,768]{1,0:T(8,128)(2,1)} %get-tuple-element.21.refs_3_, ...), custom_call_target="tpu_custom_call" | custom-call | tf_op jit(solution)/shard_map/convolve/pallas_call | solution.py:387
  93.3 23.4 %all_to_all.15.got_ref = s16[16,104,384]{2,1,0:T(8,128)(2,1)} all-to-all(s16[16,104,384]{2,1,0:T(8,128)(2,1)} %convolve.1), channel_id=1, replica_groups=mesh['lon'=16,'lat'=8] {'lon'}, dimensions={0} | all-to-all | bytes 2555904 | tf_op jit(solution)/shard_map/all_to_all | solution.py:501
  116.6 5.3 %unpack.1 = f32[96,64,96]{2,1,0:T(8,128)} custom-call(s16[16,104,384]{2,1,0:T(8,128)(2,1)} %all_to_all.15.got_ref), custom_call_target="tpu_custom_call" | custom-call | tf_op jit(solution)/shard_map/unpack/pallas_call | solution.py:409
  (2 shorter events, 0.0 us)
Async XLA Ops:
  6.4 31.3 %all-to-all-start = ((bf16[128,40,128]{2,1,0:T(8,128)(2,1)}), bf16[128,40,128]{2,1,0:T(8,128)(2,1)}, u32[]{:S(2)}, u32[]{:S(2)}) async-start(bf16[128,40,128]{2,1,0:T(8,128)(2,1)} %bitcast.9), calls=%async_computation | async-start | bytes 2621440 | tf_op jit(solution)/shard_map/all_to_all | solution.py:466
  60.4 5.9 %copy-start = (f32[1536]{0:T(1024)S(1)}, f32[1536]{0:T(1024)}, u32[]{:S(2)}) copy-start(f32[1536]{0:T(1024)} %param.17) | copy-start | bytes 18436
  60.4 25.1 %all-to-all-start.1 = ((s16[16,104,384]{2,1,0:T(8,128)(2,1)}), s16[16,104,384]{2,1,0:T(8,128)(2,1)}, u32[]{:S(2)}, u32[]{:S(2)}) async-start(s16[16,104,384]{2,1,0:T(8,128)(2,1)} %spread.1), calls=%async_computation.1 | async-start | bytes 2555904 | tf_op jit(solution)/shard_map/all_to_all | solution.py:499

commit v6 on v5

--- a/solution.py
+++ b/solution.py
@@ -347,10 +347,26 @@
         for j in range(4):
             at = (t * 4 + j) * lon_dev
             held_ref[at : at + lon_dev, :] = a[j]
-    for i in range(lon_dev):
+    row = lax.broadcasted_iota(I32, (8, LANES), 0)
+    for i in range(0, lon_dev, 8):
         for g in range(0, lats, 8):
-            picked = held_ref[pl.ds(g * lon_dev + i, 8, stride=lon_dev), :]
-            out_ref[i, g : g + 8, :] = picked[:, :levels]
+            square = [held_ref[(g + j) * lon_dev + i : (g + j) * lon_dev + i + 8, :] for j in range(8)]
+            for n, line in enumerate(transpose8(square, row)):
+                out_ref[i + n, g : g + 8, :] = line[:, :levels]
+
+
+def transpose8(square, row):
+    for step in (4, 2, 1):
+        low = (row & step) == 0
+        turned = list(square)
+        for j in range(8):
+            if j & step:
+                continue
+            a, b = square[j], square[j + step]
+            turned[j] = jnp.where(low, a, pltpu.roll(b, step, 0))
+            turned[j + step] = jnp.where(low, pltpu.roll(a, 8 - step, 0), b)
+        square = turned
+    return square
 
 
 def call_spread(got, ordered, mixer, capacity, lon_dev, lat_dev, levels, coded):

time: 124 us -> 123 us (level)
  Pallas kernels: 50.6 us -> 43.4 us
  starting transfers between devices: 16.8 us -> 23.1 us
    all_to_all x1, starting transfers between devices: 5.91 us -> 12 us  [per_device(): lax.all_to_all(field, 'lon', split_axis=0, concat_axis=0, tiled=True)]
    pallas_call x1, Pallas kernels: 22.7 us -> 16.9 us  [call_spread(): pl.pallas_call(lambda *refs: spread_kernel(capacity, lon_dev, lat_dev, le...]
where the time goes in v6:
time: 123 us; the launch traced here: 121 us
  Pallas kernels  43.4 us (35%)
  waiting for transfers between devices  26.7 us (22%)
  blocking collectives  23.4 us (19%)
  starting transfers between devices  23.1 us (19%)
  other arithmetic  2.16 us (2%)
  local copies, waits for them, and re-layouts  1.67 us (1%)
    all_to_all x1, blocking collectives, per_device(): lax.all_to_all(result, 'lon', split_axis=0, concat_axis=0, tiled=True)  23.4 us
    pallas_call x1, Pallas kernels, call_spread(): pl.pallas_call(lambda *refs: spread_kernel(capacity, lon_dev, lat_dev, le...  16.9 us
    all_to_all x1, waiting for transfers between devices, per_device(): lax.all_to_all(sent.reshape(ndev, capacity, LANES), ('lon', 'lat'), split...  14.5 us
    all_to_all x1, waiting for transfers between devices, per_device(): lax.all_to_all(field, 'lon', split_axis=0, concat_axis=0, tiled=True)  12.2 us
    all_to_all x1, starting transfers between devices, per_device(): lax.all_to_all(field, 'lon', split_axis=0, concat_axis=0, tiled=True)  12 us
    all_to_all x1, starting transfers between devices, per_device(): lax.all_to_all(sent.reshape(ndev, capacity, LANES), ('lon', 'lat'), split...  11.1 us
    pallas_call x1, Pallas kernels, call_convolve(): pl.pallas_call(conv_kernel, out_shape=jax.ShapeDtypeStruct(coded, I16), i...  7.8 us
    pallas_call x1, Pallas kernels, per_device(): pl.pallas_call(lambda *refs: prepare_kernel(lat_dev, *refs), out_shape=(j...  5.93 us
  transfers between devices with their start and end apart: 2, of which 2 were waited for; matrix products, arithmetic and copies ran while one was open for 3% of the time, Pallas kernels for 7%

profile of v6, /device:TPU:4, one launch (start us, length us, event | category | flops | bytes accessed | tf_op | source)
XLA Modules:
  0.0 121.1 jit_solution(9811489514307095611)
XLA Ops:
  0.7 5.4 %dispatch.1 = bf16[5120,128]{1,0:T(8,128)(2,1)} custom-call(s32[1]{0:T(128)S(6)} %copy.10.refs_0_, bf16[2048,128]{1,0:T(8,128)(2,1)} %refs_1_.1, s32[1,2048]{1,0:T(1,128)} %bitcast.15, s32[4,2048]{1,0:T(4,128)} %bitcast.11, s32[1,2048]{1,0:T(1,128)} %bitcast.16, bf16[96,128]{1,0:T(8,128)(2,1)} %bitcast.13), custom_call_target="tpu_custom_call" | custom-call | tf_op jit(solution)/shard_map/dispatch/pallas_call | solution.py:458
  6.0 11.1 %all-to-all-start = ((bf16[128,40,128]{2,1,0:T(8,128)(2,1)}), bf16[128,40,128]{2,1,0:T(8,128)(2,1)}, u32[]{:S(2)}, u32[]{:S(2)}) async-start(bf16[128,40,128]{2,1,0:T(8,128)(2,1)} %bitcast.9), calls=%async_computation | async-start | bytes 2621440 | tf_op jit(solution)/shard_map/all_to_all | solution.py:482
  17.1 5.9 %prepare.1 = (f32[6144,128]{1,0:T(8,128)}, bf16[256,256]{1,0:T(8,128)(2,1)}) custom-call(f32[6144,96]{1,0:T(8,128)} %bitcast.10, f32[96,96]{1,0:T(8,128)} %refs_1_.2), custom_call_target="tpu_custom_call" | custom-call | bytes 12000000 | tf_op jit(solution)/shard_map/prepare/pallas_call | solution.py:485
  23.1 14.5 %all-to-all-done = bf16[128,40,128]{2,1,0:T(8,128)(2,1)} async-done(((bf16[128,40,128]{2,1,0:T(8,128)(2,1)}), bf16[128,40,128]{2,1,0:T(8,128)(2,1)}, u32[]{:S(2)}, u32[]{:S(2)}) %all-to-all-start) | async-done | bytes 1310752 | tf_op jit(solution)/shard_map/all_to_all | solution.py:482
  37.5 16.9 %spread.1 = s16[16,104,384]{2,1,0:T(8,128)(2,1)} custom-call(bf16[5120,128]{1,0:T(8,128)(2,1)} %bitcast.5.refs_0_, f32[6144,128]{1,0:T(8,128)} %get-tuple-element.17.refs_1_, bf16[256,256]{1,0:T(8,128)(2,1)} %get-tuple-element.18.refs_2_), custom_call_target="tpu_custom_call" | custom-call | tf_op jit(solution)/shard_map/spread/pallas_call | solution.py:376
  54.5 0.0 copy-start
  54.5 12.0 %all-to-all-start.1 = ((s16[16,104,384]{2,1,0:T(8,128)(2,1)}), s16[16,104,384]{2,1,0:T(8,128)(2,1)}, u32[]{:S(2)}, u32[]{:S(2)}) async-start(s16[16,104,384]{2,1,0:T(8,128)(2,1)} %spread.1), calls=%async_computation.1 | async-start | bytes 2555904 | tf_op jit(solution)/shard_map/all_to_all | solution.py:515
  66.5 0.0 copy-done
  66.5 0.6 slice.41
  67.1 0.1 slice.42
  67.1 0.1 fusion.1
  67.2 0.5 slice.49
  67.7 0.1 slice.50
  67.8 0.1 reverse.6
  67.9 0.1 slice.55
  68.0 0.1 slice.46
  68.1 0.8 fusion
  68.8 0.1 reverse.5
  68.9 0.1 slice.54
  69.0 0.7 pad_maximum_fusion.2
  69.7 0.6 pad_maximum_fusion.kern_ref
  70.3 3.1 %toeplitz.1 = (bf16[768,768]{1,0:T(8,128)(2,1)}, bf16[768,768]{1,0:T(8,128)(2,1)}, bf16[768,768]{1,0:T(8,128)(2,1)}, bf16[768,768]{1,0:T(8,128)(2,1)}) custom-call(f32[2,768]{1,0:T(2,128)} %pad_maximum_fusion.kern_ref), custom_call_target="tpu_custom_call" | custom-call | tf_op jit(solution)/shard_map/toeplitz/pallas_call | solution.py:506
  73.4 12.2 %all-to-all-done.1.refs_0_ = s16[16,104,384]{2,1,0:T(8,128)(2,1)} async-done(((s16[16,104,384]{2,1,0:T(8,128)(2,1)}), s16[16,104,384]{2,1,0:T(8,128)(2,1)}, u32[]{:S(2)}, u32[]{:S(2)}) %all-to-all-start.1) | async-done | bytes 1277984 | tf_op jit(solution)/shard_map/all_to_all | solution.py:515
  85.6 7.8 %convolve.1 = s16[16,104,384]{2,1,0:T(8,128)(2,1)} custom-call(s16[16,104,384]{2,1,0:T(8,128)(2,1)} %all-to-all-done.1.refs_0_, bf16[768,768]{1,0:T(8,128)(2,1)} %get-tuple-element.19.refs_1_, bf16[768,768]{1,0:T(8,128)(2,1)} %get-tuple-element.20.refs_2_, bf16[768,768]{1,0:T(8,128)(2,1)} %get-tuple-element.21.refs_3_, ...), custom_call_target="tpu_custom_call" | custom-call | tf_op jit(solution)/shard_map/convolve/pallas_call | solution.py:403
  93.4 23.4 %all_to_all.15.got_ref = s16[16,104,384]{2,1,0:T(8,128)(2,1)} all-to-all(s16[16,104,384]{2,1,0:T(8,128)(2,1)} %convolve.1), channel_id=1, replica_groups=mesh['lon'=16,'lat'=8] {'lon'}, dimensions={0} | all-to-all | bytes 2555904 | tf_op jit(solution)/shard_map/all_to_all | solution.py:517
  116.9 4.3 %unpack.1 = f32[96,64,96]{2,1,0:T(8,128)} custom-call(s16[16,104,384]{2,1,0:T(8,128)(2,1)} %all_to_all.15.got_ref), custom_call_target="tpu_custom_call" | custom-call | tf_op jit(solution)/shard_map/unpack/pallas_call | solution.py:425
  (2 shorter events, 0.0 us)
Async XLA Ops:
  6.0 31.5 %all-to-all-start = ((bf16[128,40,128]{2,1,0:T(8,128)(2,1)}), bf16[128,40,128]{2,1,0:T(8,128)(2,1)}, u32[]{:S(2)}, u32[]{:S(2)}) async-start(bf16[128,40,128]{2,1,0:T(8,128)(2,1)} %bitcast.9), calls=%async_computation | async-start | bytes 2621440 | tf_op jit(solution)/shard_map/all_to_all | solution.py:482
  54.5 12.0 %copy-start = (f32[1536]{0:T(1024)S(1)}, f32[1536]{0:T(1024)}, u32[]{:S(2)}) copy-start(f32[1536]{0:T(1024)} %param.17) | copy-start | bytes 18436
  54.5 31.2 %all-to-all-start.1 = ((s16[16,104,384]{2,1,0:T(8,128)(2,1)}), s16[16,104,384]{2,1,0:T(8,128)(2,1)}, u32[]{:S(2)}, u32[]{:S(2)}) async-start(s16[16,104,384]{2,1,0:T(8,128)(2,1)} %spread.1), calls=%async_computation.1 | async-start | bytes 2555904 | tf_op jit(solution)/shard_map/all_to_all | solution.py:515

commit v7 on v6

--- a/solution.py
+++ b/solution.py
@@ -76,16 +76,29 @@
     earlier = (
         lax.broadcasted_iota(I32, (block, block), 0) < lax.broadcasted_iota(I32, (block, block), 1)
     ).astype(F32).astype(BF16)
-    carry = jnp.zeros((ndev, 1), F32)
-    for b in range(nrows // block):
+
+
+    def hits(b):
         cols = slice(b * block, (b + 1) * block)
         position = lax.broadcasted_iota(I32, (1, block), 1) + b * block
         live = position < n_live
         owner = owner_ref[:, cols]
-        hit = ((owner_ids == owner) & live).astype(F32)
-        before = jnp.dot(hit.astype(BF16), earlier, preferred_element_type=F32) + carry
-        rank = jnp.sum(hit * before, axis=0, keepdims=True).astype(I32)
-        carry = carry + jnp.sum(hit, axis=1, keepdims=True)
+        hit = (owner_ids == owner) & live
+        full = count_ref[:, cols] > 2
+        return live, owner, (hit & full).astype(F32), (hit & ~full).astype(F32)
+
+    full_carry = jnp.zeros((ndev, 1), F32)
+    rest_carry = full_carry
+    for b in range(nrows // block):
+        rest_carry = rest_carry + jnp.sum(hits(b)[2], axis=1, keepdims=True)
+    for b in range(nrows // block):
+        live, owner, full, rest = hits(b)
+        both = jnp.concatenate([full, rest], axis=0).astype(BF16)
+        before = jnp.dot(both, earlier, preferred_element_type=F32)
+        rank = full * (before[:ndev] + full_carry) + rest * (before[ndev:] + rest_carry)
+        rank = jnp.sum(rank, axis=0, keepdims=True).astype(I32)
+        full_carry = full_carry + jnp.sum(full, axis=1, keepdims=True)
+        rest_carry = rest_carry + jnp.sum(rest, axis=1, keepdims=True)
         slot = jnp.where(live, owner * capacity + rank, slots)
         for i in range(block // LANES):
             row = b * (block // LANES) + i
@@ -103,9 +116,8 @@
         used = lax.broadcasted_iota(I32, (foot, block), 0) < count
         lon = jnp.where(used, cell // 64, 0).astype(F32)
         lat = jnp.where(used, cell % 64, 64).astype(F32)
-        rest = jnp.where(
-            lax.broadcasted_iota(I32, (LANES - levels - 2 * foot, block), 0) == 0, 1.0, 0.0
-        )
+        kind = lax.broadcasted_iota(I32, (LANES - levels - 2 * foot, block), 0)
+        rest = jnp.where((kind == 0) | ((kind == 1) & (count > 2)), 1.0, 0.0)
         payload = jnp.concatenate([share, jnp.concatenate([lon, lat], axis=0), rest], axis=0)
         pay_ref[cols, :] = payload.T
     even_ref[...] = jnp.zeros_like(even_ref)
@@ -164,7 +176,7 @@
     span = foot * chunk
     row_i = lax.broadcasted_iota(I32, (LANES, LANES), 0) - levels
     lane_i = lax.broadcasted_iota(I32, (LANES, LANES), 1)
-    pick = (row_i >= 0) & (row_i <= 2 * foot) & (row_i == lane_i // chunk)
+    pick = (row_i >= 0) & (row_i <= 2 * foot + 1) & (row_i == lane_i // chunk)
     pick = jnp.where(pick, 1.0, 0.0).astype(BF16)
     block = 256
     own = lax.broadcasted_iota(I32, (block, LANES), 0) % chunk
@@ -185,7 +197,7 @@
         table = jnp.where(is_cell, table + turned * float(lon_dev), table)
         at = b * (block // chunk)
         fields_v[at : at + block // chunk, :] = table
-    lanes = list(range(span)) + [2 * span]
+    lanes = list(range(span)) + [2 * span, 2 * span + chunk]
     for i in range(slots // chunk // LANES):
         cols = slice(i * LANES, (i + 1) * LANES)
         turned = fields_v[cols, :].T.astype(I32)
@@ -205,18 +217,29 @@
         n_chunks = tables[span][base]
         for c in range(1, per_source):
             n_chunks = n_chunks + tables[span][base + c]
-
-        def one_chunk(c, _):
+        n_full = tables[span + 1][base]
+        for c in range(1, per_source):
+            n_full = n_full + tables[span + 1][base + c]
+
+        def one_chunk(c, used):
             first = pl.multiple_of(c * chunk, chunk)
             for u in range(chunk):
                 row = share_ref[pl.ds(first + u, 1), :]
-                for f in range(foot):
+                for f in range(used):
                     cell = tables[f * chunk + u][c]
-                    acc = accs[(u * foot + f) % N_ACC]
+                    acc = accs[(u * used + f) % N_ACC]
                     acc[pl.ds(cell, 1), :] = acc[pl.ds(cell, 1), :] + row
+
+        def full_chunk(c, _):
+            one_chunk(c, foot)
             return 0
 
-        lax.fori_loop(base, base + n_chunks, one_chunk, 0)
+        def half_chunk(c, _):
+            one_chunk(c, foot // 2)
+            return 0
+
+        lax.fori_loop(base, base + n_full, full_chunk, 0)
+        lax.fori_loop(base + n_full, base + n_chunks, half_chunk, 0)
         return 0
 
     lax.fori_loop(0, ndev, one_source, 0)
@@ -383,13 +406,13 @@
             pltpu.VMEM(coded, I16),
             pltpu.VMEM((slots, LANES), F32),
             pltpu.VMEM((slots // 8, LANES), F32),
-            pltpu.VMEM((33, 1, slots // 8), I32),
-            pltpu.SemaphoreType.DMA((34,)),
+            pltpu.VMEM((34, 1, slots // 8), I32),
+            pltpu.SemaphoreType.DMA((35,)),
             pltpu.SemaphoreType.DMA((4,)),
             pltpu.SemaphoreType.DMA((coded[0],)),
         ]
         + [acc] * N_ACC
-        + [pltpu.SMEM((slots // 8,), I32)] * 33,
+        + [pltpu.SMEM((slots // 8,), I32)] * 34,
         compiler_params=params(),
         name="spread",
     )(got, ordered, mixer)

time: 123 us -> 122 us (level)
  starting transfers between devices: 23.1 us -> 20.4 us
  Pallas kernels: 43.4 us -> 45.8 us
    all_to_all x1, starting transfers between devices: 12 us -> 9.62 us  [per_device(): lax.all_to_all(field, 'lon', split_axis=0, concat_axis=0, tiled=True)]
    pallas_call x1, Pallas kernels: 16.9 us -> 18.2 us  [call_spread(): pl.pallas_call(lambda *refs: spread_kernel(capacity, lon_dev, lat_dev, le...]
where the time goes in v7:
time: 122 us; the launch traced here: 121 us
  Pallas kernels  45.8 us (38%)
  waiting for transfers between devices  26.7 us (22%)
  blocking collectives  23.4 us (19%)
  starting transfers between devices  20.4 us (17%)
  other arithmetic  2.16 us (2%)
  local copies, waits for them, and re-layouts  1.67 us (1%)
    all_to_all x1, blocking collectives, per_device(): lax.all_to_all(result, 'lon', split_axis=0, concat_axis=0, tiled=True)  23.4 us
    pallas_call x1, Pallas kernels, call_spread(): pl.pallas_call(lambda *refs: spread_kernel(capacity, lon_dev, lat_dev, le...  18.2 us
    all_to_all x1, waiting for transfers between devices, per_device(): lax.all_to_all(sent.reshape(ndev, capacity, LANES), ('lon', 'lat'), split...  14.5 us
    all_to_all x1, waiting for transfers between devices, per_device(): lax.all_to_all(field, 'lon', split_axis=0, concat_axis=0, tiled=True)  12.2 us
    all_to_all x1, starting transfers between devices, per_device(): lax.all_to_all(sent.reshape(ndev, capacity, LANES), ('lon', 'lat'), split...  10.8 us
    all_to_all x1, starting transfers between devices, per_device(): lax.all_to_all(field, 'lon', split_axis=0, concat_axis=0, tiled=True)  9.62 us
    pallas_call x1, Pallas kernels, call_convolve(): pl.pallas_call(conv_kernel, out_shape=jax.ShapeDtypeStruct(coded, I16), i...  7.8 us
    pallas_call x1, Pallas kernels, per_device(): pl.pallas_call(lambda *refs: dispatch_kernel(capacity, *refs), out_shape=...  6.44 us
  transfers between devices with their start and end apart: 2, of which 2 were waited for; matrix products, arithmetic and copies ran while one was open for 3% of the time, Pallas kernels for 7%

profile of v7, /device:TPU:4, one launch (start us, length us, event | category | flops | bytes accessed | tf_op | source)
XLA Modules:
  0.0 120.8 jit_solution(4796437767489813427)
XLA Ops:
  0.7 6.4 %dispatch.1 = bf16[5120,128]{1,0:T(8,128)(2,1)} custom-call(s32[1]{0:T(128)S(6)} %copy.10.refs_0_, bf16[2048,128]{1,0:T(8,128)(2,1)} %refs_1_.1, s32[1,2048]{1,0:T(1,128)} %bitcast.15, s32[4,2048]{1,0:T(4,128)} %bitcast.11, s32[1,2048]{1,0:T(1,128)} %bitcast.16, bf16[96,128]{1,0:T(8,128)(2,1)} %bitcast.13), custom_call_target="tpu_custom_call" | custom-call | tf_op jit(solution)/shard_map/dispatch/pallas_call | solution.py:481
  7.1 10.8 %all-to-all-start = ((bf16[128,40,128]{2,1,0:T(8,128)(2,1)}), bf16[128,40,128]{2,1,0:T(8,128)(2,1)}, u32[]{:S(2)}, u32[]{:S(2)}) async-start(bf16[128,40,128]{2,1,0:T(8,128)(2,1)} %bitcast.9), calls=%async_computation | async-start | bytes 2621440 | tf_op jit(solution)/shard_map/all_to_all | solution.py:505
  17.9 5.9 %prepare.1 = (f32[6144,128]{1,0:T(8,128)}, bf16[256,256]{1,0:T(8,128)(2,1)}) custom-call(f32[6144,96]{1,0:T(8,128)} %bitcast.10, f32[96,96]{1,0:T(8,128)} %refs_1_.2), custom_call_target="tpu_custom_call" | custom-call | bytes 12000000 | tf_op jit(solution)/shard_map/prepare/pallas_call | solution.py:508
  23.8 14.5 %all-to-all-done = bf16[128,40,128]{2,1,0:T(8,128)(2,1)} async-done(((bf16[128,40,128]{2,1,0:T(8,128)(2,1)}), bf16[128,40,128]{2,1,0:T(8,128)(2,1)}, u32[]{:S(2)}, u32[]{:S(2)}) %all-to-all-start) | async-done | bytes 1310752 | tf_op jit(solution)/shard_map/all_to_all | solution.py:505
  38.3 18.2 %spread.1 = s16[16,104,384]{2,1,0:T(8,128)(2,1)} custom-call(bf16[5120,128]{1,0:T(8,128)(2,1)} %bitcast.5.refs_0_, f32[6144,128]{1,0:T(8,128)} %get-tuple-element.17.refs_1_, bf16[256,256]{1,0:T(8,128)(2,1)} %get-tuple-element.18.refs_2_), custom_call_target="tpu_custom_call" | custom-call | tf_op jit(solution)/shard_map/spread/pallas_call | solution.py:399
  56.5 0.0 copy-start
  56.5 9.6 %all-to-all-start.1 = ((s16[16,104,384]{2,1,0:T(8,128)(2,1)}), s16[16,104,384]{2,1,0:T(8,128)(2,1)}, u32[]{:S(2)}, u32[]{:S(2)}) async-start(s16[16,104,384]{2,1,0:T(8,128)(2,1)} %spread.1), calls=%async_computation.1 | async-start | bytes 2555904 | tf_op jit(solution)/shard_map/all_to_all | solution.py:538
  66.2 0.0 copy-done
  66.2 0.6 slice.41
  66.8 0.1 slice.42
  66.8 0.1 fusion.1
  66.9 0.5 slice.49
  67.4 0.1 slice.50
  67.5 0.1 reverse.6
  67.6 0.1 slice.55
  67.7 0.1 slice.46
  67.7 0.8 fusion
  68.5 0.1 reverse.5
  68.6 0.1 slice.54
  68.7 0.7 pad_maximum_fusion.2
  69.4 0.6 pad_maximum_fusion.kern_ref
  70.0 3.1 %toeplitz.1 = (bf16[768,768]{1,0:T(8,128)(2,1)}, bf16[768,768]{1,0:T(8,128)(2,1)}, bf16[768,768]{1,0:T(8,128)(2,1)}, bf16[768,768]{1,0:T(8,128)(2,1)}) custom-call(f32[2,768]{1,0:T(2,128)} %pad_maximum_fusion.kern_ref), custom_call_target="tpu_custom_call" | custom-call | tf_op jit(solution)/shard_map/toeplitz/pallas_call | solution.py:529
  73.1 12.2 %all-to-all-done.1.refs_0_ = s16[16,104,384]{2,1,0:T(8,128)(2,1)} async-done(((s16[16,104,384]{2,1,0:T(8,128)(2,1)}), s16[16,104,384]{2,1,0:T(8,128)(2,1)}, u32[]{:S(2)}, u32[]{:S(2)}) %all-to-all-start.1) | async-done | bytes 1277984 | tf_op jit(solution)/shard_map/all_to_all | solution.py:538
  85.3 7.8 %convolve.1 = s16[16,104,384]{2,1,0:T(8,128)(2,1)} custom-call(s16[16,104,384]{2,1,0:T(8,128)(2,1)} %all-to-all-done.1.refs_0_, bf16[768,768]{1,0:T(8,128)(2,1)} %get-tuple-element.19.refs_1_, bf16[768,768]{1,0:T(8,128)(2,1)} %get-tuple-element.20.refs_2_, bf16[768,768]{1,0:T(8,128)(2,1)} %get-tuple-element.21.refs_3_, ...), custom_call_target="tpu_custom_call" | custom-call | tf_op jit(solution)/shard_map/convolve/pallas_call | solution.py:426
  93.1 23.4 %all_to_all.15.got_ref = s16[16,104,384]{2,1,0:T(8,128)(2,1)} all-to-all(s16[16,104,384]{2,1,0:T(8,128)(2,1)} %convolve.1), channel_id=1, replica_groups=mesh['lon'=16,'lat'=8] {'lon'}, dimensions={0} | all-to-all | bytes 2555904 | tf_op jit(solution)/shard_map/all_to_all | solution.py:540
  116.5 4.3 %unpack.1 = f32[96,64,96]{2,1,0:T(8,128)} custom-call(s16[16,104,384]{2,1,0:T(8,128)(2,1)} %all_to_all.15.got_ref), custom_call_target="tpu_custom_call" | custom-call | tf_op jit(solution)/shard_map/unpack/pallas_call | solution.py:448
  (2 shorter events, 0.0 us)
Async XLA Ops:
  7.1 31.2 %all-to-all-start = ((bf16[128,40,128]{2,1,0:T(8,128)(2,1)}), bf16[128,40,128]{2,1,0:T(8,128)(2,1)}, u32[]{:S(2)}, u32[]{:S(2)}) async-start(bf16[128,40,128]{2,1,0:T(8,128)(2,1)} %bitcast.9), calls=%async_computation | async-start | bytes 2621440 | tf_op jit(solution)/shard_map/all_to_all | solution.py:505
  56.5 9.6 %copy-start = (f32[1536]{0:T(1024)S(1)}, f32[1536]{0:T(1024)}, u32[]{:S(2)}) copy-start(f32[1536]{0:T(1024)} %param.17) | copy-start | bytes 18436
  56.5 28.8 %all-to-all-start.1 = ((s16[16,104,384]{2,1,0:T(8,128)(2,1)}), s16[16,104,384]{2,1,0:T(8,128)(2,1)}, u32[]{:S(2)}, u32[]{:S(2)}) async-start(s16[16,104,384]{2,1,0:T(8,128)(2,1)} %spread.1), calls=%async_computation.1 | async-start | bytes 2555904 | tf_op jit(solution)/shard_map/all_to_all | solution.py:538

commit v8 on v7

--- a/solution.py
+++ b/solution.py
@@ -24,7 +24,7 @@
     return pltpu.CompilerParams(vmem_limit_bytes=mib * 1024 * 1024)
 
 
-def quantise(tiles, out_ref, place):
+def quantise(tiles, out_ref, place, first=0):
     rows = tiles[0].shape[0]
     for k, tile in enumerate(tiles):
         top = jnp.max(jnp.abs(tile), axis=0, keepdims=True)
@@ -33,7 +33,7 @@
         digits = jnp.round(tile * factor)
         codes = jnp.broadcast_to(power, (CODE_ROWS, LANES))
         whole = jnp.concatenate([digits, codes], axis=0).astype(I32)
-        out_ref[place, :, k * LANES : (k + 1) * LANES] = whole.astype(I16)
+        out_ref[place, :, first + k * LANES : first + (k + 1) * LANES] = whole.astype(I16)
 
 
 def dequantise(in_ref, place):
@@ -176,8 +176,9 @@
     span = foot * chunk
     row_i = lax.broadcasted_iota(I32, (LANES, LANES), 0) - levels
     lane_i = lax.broadcasted_iota(I32, (LANES, LANES), 1)
-    pick = (row_i >= 0) & (row_i <= 2 * foot + 1) & (row_i == lane_i // chunk)
-    pick = jnp.where(pick, 1.0, 0.0).astype(BF16)
+    group = lane_i // chunk
+    pick = jnp.where((row_i >= 0) & (row_i <= 2 * foot) & (row_i == group), 1.0, 0.0)
+    pick = jnp.where((row_i == 2 * foot + 1) & (group == 2 * foot), 8.0, pick).astype(BF16)
     block = 256
     own = lax.broadcasted_iota(I32, (block, LANES), 0) % chunk
     own = own == lax.broadcasted_iota(I32, (block, LANES), 1) % chunk
@@ -197,7 +198,7 @@
         table = jnp.where(is_cell, table + turned * float(lon_dev), table)
         at = b * (block // chunk)
         fields_v[at : at + block // chunk, :] = table
-    lanes = list(range(span)) + [2 * span, 2 * span + chunk]
+    lanes = list(range(span)) + [2 * span]
     for i in range(slots // chunk // LANES):
         cols = slice(i * LANES, (i + 1) * LANES)
         turned = fields_v[cols, :].T.astype(I32)
@@ -214,12 +215,10 @@
 
     def one_source(s, _):
         base = s * per_source
-        n_chunks = tables[span][base]
+        code = tables[span][base]
         for c in range(1, per_source):
-            n_chunks = n_chunks + tables[span][base + c]
-        n_full = tables[span + 1][base]
-        for c in range(1, per_source):
-            n_full = n_full + tables[span + 1][base + c]
+            code = code + tables[span][base + c]
+        n_chunks, n_full = code & 7, code >> 3
 
         def one_chunk(c, used):
             first = pl.multiple_of(c * chunk, chunk)
@@ -318,6 +317,7 @@
     rows = got_ref.shape[1] - CODE_ROWS
     width = got_ref.shape[2]
     half = n_lon // 2
+    parts = ((0, 2 * LANES), (2 * LANES, width))
     gets = [
         pltpu.make_async_copy(got_hbm.at[s], got_ref.at[s], in_sems.at[s]) for s in range(n_lon)
     ]
@@ -334,23 +334,33 @@
         a = dequantise(got_ref, s)
         b = dequantise(got_ref, s + half)
         at = slice(s * rows, (s + 1) * rows)
-        xp[at, :width], xp[at, width:] = split(a + b)
-        xm[at, :width], xm[at, width:] = split(a - b)
-    for i, (th, tl, x, y) in enumerate(((ph_ref, pl_ref, xp, yp), (mh_ref, ml_ref, xm, ym))):
-        loads[2 * i].wait()
-        loads[2 * i + 1].wait()
-        both = jnp.dot(th[...], x[...], preferred_element_type=F32)
-        rest = jnp.dot(tl[...], x[:, :width], preferred_element_type=F32)
-        y[...] = both[:, :width] + (both[:, width:] + rest)
+        for x, value in ((xp, a + b), (xm, a - b)):
+            high, low = split(value)
+            for begin, end in parts:
+                x[at, 2 * begin : begin + end] = high[:, begin:end]
+                x[at, begin + end : 2 * end] = low[:, begin:end]
     puts = []
-    for s in range(half):
-        at = slice(s * rows, (s + 1) * rows)
-        plus, minus = yp[at, :], ym[at, :]
-        for place, y in ((s, 0.5 * (plus + minus)), (s + half, 0.5 * (plus - minus))):
-            quantise([y[:, k : k + LANES] for k in range(0, width, LANES)], out_ref, place)
-            put = pltpu.make_async_copy(out_ref.at[place], out_hbm.at[place], out_sems.at[place])
-            put.start()
-            puts.append(put)
+    for begin, end in parts:
+        wide = end - begin
+        for i, (th, tl, x, y) in enumerate(((ph_ref, pl_ref, xp, yp), (mh_ref, ml_ref, xm, ym))):
+            if begin == 0:
+                loads[2 * i].wait()
+                loads[2 * i + 1].wait()
+            both = jnp.dot(th[...], x[:, 2 * begin : 2 * end], preferred_element_type=F32)
+            rest = jnp.dot(tl[...], x[:, 2 * begin : begin + end], preferred_element_type=F32)
+            y[:, begin:end] = both[:, :wide] + (both[:, wide:] + rest)
+        for s in range(half):
+            at = slice(s * rows, (s + 1) * rows)
+            plus, minus = yp[at, begin:end], ym[at, begin:end]
+            for place, y in ((s, 0.5 * (plus + minus)), (s + half, 0.5 * (plus - minus))):
+                tiles = [y[:, k : k + LANES] for k in range(0, wide, LANES)]
+                quantise(tiles, out_ref, place, begin)
+                if end == width:
+                    put = pltpu.make_async_copy(
+                        out_ref.at[place], out_hbm.at[place], out_sems.at[place]
+                    )
+                    put.start()
+                    puts.append(put)
     for put in puts:
         put.wait()
 
@@ -406,13 +416,13 @@
             pltpu.VMEM(coded, I16),
             pltpu.VMEM((slots, LANES), F32),
             pltpu.VMEM((slots // 8, LANES), F32),
-            pltpu.VMEM((34, 1, slots // 8), I32),
-            pltpu.SemaphoreType.DMA((35,)),
+            pltpu.VMEM((33, 1, slots // 8), I32),
+            pltpu.SemaphoreType.DMA((34,)),
             pltpu.SemaphoreType.DMA((4,)),
             pltpu.SemaphoreType.DMA((coded[0],)),
         ]
         + [acc] * N_ACC
-        + [pltpu.SMEM((slots // 8,), I32)] * 34,
+        + [pltpu.SMEM((slots // 8,), I32)] * 33,
         compiler_params=params(),
         name="spread",
     )(got, ordered, mixer)

time: 122 us -> 123 us (level)
    pallas_call x1, Pallas kernels: 7.8 us -> 9.06 us  [call_convolve(): pl.pallas_call(conv_kernel, out_shape=jax.ShapeDtypeStruct(coded, I16), i...]
where the time goes in v8:
time: 123 us; the launch traced here: 121 us
  Pallas kernels  46.1 us (37%)
  waiting for transfers between devices  26.7 us (22%)
  blocking collectives  23.4 us (19%)
  starting transfers between devices  20.4 us (17%)
  other arithmetic  2.16 us (2%)
  local copies, waits for them, and re-layouts  1.67 us (1%)
    all_to_all x1, blocking collectives, per_device(): lax.all_to_all(result, 'lon', split_axis=0, concat_axis=0, tiled=True)  23.4 us
    pallas_call x1, Pallas kernels, call_spread(): pl.pallas_call(lambda *refs: spread_kernel(capacity, lon_dev, lat_dev, le...  17.7 us
    all_to_all x1, waiting for transfers between devices, per_device(): lax.all_to_all(sent.reshape(ndev, capacity, LANES), ('lon', 'lat'), split...  14.5 us
    all_to_all x1, waiting for transfers between devices, per_device(): lax.all_to_all(field, 'lon', split_axis=0, concat_axis=0, tiled=True)  12.2 us
    all_to_all x1, starting transfers between devices, per_device(): lax.all_to_all(sent.reshape(ndev, capacity, LANES), ('lon', 'lat'), split...  11.1 us
    all_to_all x1, starting transfers between devices, per_device(): lax.all_to_all(field, 'lon', split_axis=0, concat_axis=0, tiled=True)  9.27 us
    pallas_call x1, Pallas kernels, call_convolve(): pl.pallas_call(conv_kernel, out_shape=jax.ShapeDtypeStruct(coded, I16), i...  9.06 us
    pallas_call x1, Pallas kernels, per_device(): pl.pallas_call(lambda *refs: dispatch_kernel(capacity, *refs), out_shape=...  6 us
  transfers between devices with their start and end apart: 2, of which 2 were waited for; matrix products, arithmetic and copies ran while one was open for 3% of the time, Pallas kernels for 7%

profile of v8, /device:TPU:4, one launch (start us, length us, event | category | flops | bytes accessed | tf_op | source)
XLA Modules:
  0.0 121.1 jit_solution(11758148629828046414)
XLA Ops:
  0.7 6.0 %dispatch.1 = bf16[5120,128]{1,0:T(8,128)(2,1)} custom-call(s32[1]{0:T(128)S(6)} %copy.10.refs_0_, bf16[2048,128]{1,0:T(8,128)(2,1)} %refs_1_.1, s32[1,2048]{1,0:T(1,128)} %bitcast.15, s32[4,2048]{1,0:T(4,128)} %bitcast.11, s32[1,2048]{1,0:T(1,128)} %bitcast.16, bf16[96,128]{1,0:T(8,128)(2,1)} %bitcast.13), custom_call_target="tpu_custom_call" | custom-call | tf_op jit(solution)/shard_map/dispatch/pallas_call | solution.py:491
  6.7 11.1 %all-to-all-start = ((bf16[128,40,128]{2,1,0:T(8,128)(2,1)}), bf16[128,40,128]{2,1,0:T(8,128)(2,1)}, u32[]{:S(2)}, u32[]{:S(2)}) async-start(bf16[128,40,128]{2,1,0:T(8,128)(2,1)} %bitcast.9), calls=%async_computation | async-start | bytes 2621440 | tf_op jit(solution)/shard_map/all_to_all | solution.py:515
  17.8 5.9 %prepare.1 = (f32[6144,128]{1,0:T(8,128)}, bf16[256,256]{1,0:T(8,128)(2,1)}) custom-call(f32[6144,96]{1,0:T(8,128)} %bitcast.10, f32[96,96]{1,0:T(8,128)} %refs_1_.2), custom_call_target="tpu_custom_call" | custom-call | bytes 12000000 | tf_op jit(solution)/shard_map/prepare/pallas_call | solution.py:518
  23.7 14.5 %all-to-all-done = bf16[128,40,128]{2,1,0:T(8,128)(2,1)} async-done(((bf16[128,40,128]{2,1,0:T(8,128)(2,1)}), bf16[128,40,128]{2,1,0:T(8,128)(2,1)}, u32[]{:S(2)}, u32[]{:S(2)}) %all-to-all-start) | async-done | bytes 1310752 | tf_op jit(solution)/shard_map/all_to_all | solution.py:515
  38.2 17.7 %spread.1 = s16[16,104,384]{2,1,0:T(8,128)(2,1)} custom-call(bf16[5120,128]{1,0:T(8,128)(2,1)} %bitcast.5.refs_0_, f32[6144,128]{1,0:T(8,128)} %get-tuple-element.17.refs_1_, bf16[256,256]{1,0:T(8,128)(2,1)} %get-tuple-element.18.refs_2_), custom_call_target="tpu_custom_call" | custom-call | tf_op jit(solution)/shard_map/spread/pallas_call | solution.py:409
  55.9 0.0 copy-start
  55.9 9.3 %all-to-all-start.1 = ((s16[16,104,384]{2,1,0:T(8,128)(2,1)}), s16[16,104,384]{2,1,0:T(8,128)(2,1)}, u32[]{:S(2)}, u32[]{:S(2)}) async-start(s16[16,104,384]{2,1,0:T(8,128)(2,1)} %spread.1), calls=%async_computation.1 | async-start | bytes 2555904 | tf_op jit(solution)/shard_map/all_to_all | solution.py:548
  65.2 0.0 copy-done
  65.2 0.6 slice.41
  65.8 0.1 slice.42
  65.9 0.1 fusion.1
  66.0 0.5 slice.49
  66.5 0.1 slice.50
  66.5 0.1 reverse.6
  66.6 0.1 slice.55
  66.7 0.1 slice.46
  66.8 0.8 fusion
  67.6 0.1 reverse.5
  67.6 0.1 slice.54
  67.7 0.7 pad_maximum_fusion.2
  68.5 0.6 pad_maximum_fusion.kern_ref
  69.1 3.1 %toeplitz.1 = (bf16[768,768]{1,0:T(8,128)(2,1)}, bf16[768,768]{1,0:T(8,128)(2,1)}, bf16[768,768]{1,0:T(8,128)(2,1)}, bf16[768,768]{1,0:T(8,128)(2,1)}) custom-call(f32[2,768]{1,0:T(2,128)} %pad_maximum_fusion.kern_ref), custom_call_target="tpu_custom_call" | custom-call | tf_op jit(solution)/shard_map/toeplitz/pallas_call | solution.py:539
  72.1 12.2 %all-to-all-done.1.refs_0_ = s16[16,104,384]{2,1,0:T(8,128)(2,1)} async-done(((s16[16,104,384]{2,1,0:T(8,128)(2,1)}), s16[16,104,384]{2,1,0:T(8,128)(2,1)}, u32[]{:S(2)}, u32[]{:S(2)}) %all-to-all-start.1) | async-done | bytes 1277984 | tf_op jit(solution)/shard_map/all_to_all | solution.py:548
  84.4 9.1 %convolve.1 = s16[16,104,384]{2,1,0:T(8,128)(2,1)} custom-call(s16[16,104,384]{2,1,0:T(8,128)(2,1)} %all-to-all-done.1.refs_0_, bf16[768,768]{1,0:T(8,128)(2,1)} %get-tuple-element.19.refs_1_, bf16[768,768]{1,0:T(8,128)(2,1)} %get-tuple-element.20.refs_2_, bf16[768,768]{1,0:T(8,128)(2,1)} %get-tuple-element.21.refs_3_, ...), custom_call_target="tpu_custom_call" | custom-call | tf_op jit(solution)/shard_map/convolve/pallas_call | solution.py:436
  93.4 23.4 %all_to_all.15.got_ref = s16[16,104,384]{2,1,0:T(8,128)(2,1)} all-to-all(s16[16,104,384]{2,1,0:T(8,128)(2,1)} %convolve.1), channel_id=1, replica_groups=mesh['lon'=16,'lat'=8] {'lon'}, dimensions={0} | all-to-all | bytes 2555904 | tf_op jit(solution)/shard_map/all_to_all | solution.py:550
  116.8 4.3 %unpack.1 = f32[96,64,96]{2,1,0:T(8,128)} custom-call(s16[16,104,384]{2,1,0:T(8,128)(2,1)} %all_to_all.15.got_ref), custom_call_target="tpu_custom_call" | custom-call | tf_op jit(solution)/shard_map/unpack/pallas_call | solution.py:458
  (2 shorter events, 0.0 us)
Async XLA Ops:
  6.7 31.5 %all-to-all-start = ((bf16[128,40,128]{2,1,0:T(8,128)(2,1)}), bf16[128,40,128]{2,1,0:T(8,128)(2,1)}, u32[]{:S(2)}, u32[]{:S(2)}) async-start(bf16[128,40,128]{2,1,0:T(8,128)(2,1)} %bitcast.9), calls=%async_computation | async-start | bytes 2621440 | tf_op jit(solution)/shard_map/all_to_all | solution.py:515
  55.9 9.3 %copy-start = (f32[1536]{0:T(1024)S(1)}, f32[1536]{0:T(1024)}, u32[]{:S(2)}) copy-start(f32[1536]{0:T(1024)} %param.17) | copy-start | bytes 18436
  55.9 28.4 %all-to-all-start.1 = ((s16[16,104,384]{2,1,0:T(8,128)(2,1)}), s16[16,104,384]{2,1,0:T(8,128)(2,1)}, u32[]{:S(2)}, u32[]{:S(2)}) async-start(s16[16,104,384]{2,1,0:T(8,128)(2,1)} %spread.1), calls=%async_computation.1 | async-start | bytes 2555904 | tf_op jit(solution)/shard_map/all_to_all | solution.py:548

commit v9 on v7

--- a/solution.py
+++ b/solution.py
@@ -176,8 +176,9 @@
     span = foot * chunk
     row_i = lax.broadcasted_iota(I32, (LANES, LANES), 0) - levels
     lane_i = lax.broadcasted_iota(I32, (LANES, LANES), 1)
-    pick = (row_i >= 0) & (row_i <= 2 * foot + 1) & (row_i == lane_i // chunk)
-    pick = jnp.where(pick, 1.0, 0.0).astype(BF16)
+    group = lane_i // chunk
+    pick = jnp.where((row_i >= 0) & (row_i <= 2 * foot) & (row_i == group), 1.0, 0.0)
+    pick = jnp.where((row_i == 2 * foot + 1) & (group == 2 * foot), 8.0, pick).astype(BF16)
     block = 256
     own = lax.broadcasted_iota(I32, (block, LANES), 0) % chunk
     own = own == lax.broadcasted_iota(I32, (block, LANES), 1) % chunk
@@ -197,7 +198,7 @@
         table = jnp.where(is_cell, table + turned * float(lon_dev), table)
         at = b * (block // chunk)
         fields_v[at : at + block // chunk, :] = table
-    lanes = list(range(span)) + [2 * span, 2 * span + chunk]
+    lanes = list(range(span)) + [2 * span]
     for i in range(slots // chunk // LANES):
         cols = slice(i * LANES, (i + 1) * LANES)
         turned = fields_v[cols, :].T.astype(I32)
@@ -214,12 +215,10 @@
 
     def one_source(s, _):
         base = s * per_source
-        n_chunks = tables[span][base]
+        code = tables[span][base]
         for c in range(1, per_source):
-            n_chunks = n_chunks + tables[span][base + c]
-        n_full = tables[span + 1][base]
-        for c in range(1, per_source):
-            n_full = n_full + tables[span + 1][base + c]
+            code = code + tables[span][base + c]
+        n_chunks, n_full = code & 7, code >> 3
 
         def one_chunk(c, used):
             first = pl.multiple_of(c * chunk, chunk)
@@ -406,13 +405,13 @@
             pltpu.VMEM(coded, I16),
             pltpu.VMEM((slots, LANES), F32),
             pltpu.VMEM((slots // 8, LANES), F32),
-            pltpu.VMEM((34, 1, slots // 8), I32),
-            pltpu.SemaphoreType.DMA((35,)),
+            pltpu.VMEM((33, 1, slots // 8), I32),
+            pltpu.SemaphoreType.DMA((34,)),
             pltpu.SemaphoreType.DMA((4,)),
             pltpu.SemaphoreType.DMA((coded[0],)),
         ]
         + [acc] * N_ACC
-        + [pltpu.SMEM((slots // 8,), I32)] * 34,
+        + [pltpu.SMEM((slots // 8,), I32)] * 33,
         compiler_params=params(),
         name="spread",
     )(got, ordered, mixer)

time: 122 us -> 122 us (level)
  the two profiles are of different devices: /device:TPU:4 before, /device:TPU:1 now
where the time goes in v9:
time: 122 us
  Pallas kernels  51.1 us (42%)
  waiting for transfers between devices  25.8 us (21%)
  blocking collectives  23.3 us (19%)
  starting transfers between devices  17.1 us (14%)
  other arithmetic  2.16 us (2%)
  local copies, waits for them, and re-layouts  1.67 us (1%)
    pallas_call x1, Pallas kernels, call_spread(): pl.pallas_call(lambda *refs: spread_kernel(capacity, lon_dev, lat_dev, le...  24.2 us
    all_to_all x1, blocking collectives, per_device(): lax.all_to_all(result, 'lon', split_axis=0, concat_axis=0, tiled=True)  23.3 us
    all_to_all x1, waiting for transfers between devices, per_device(): lax.all_to_all(sent.reshape(ndev, capacity, LANES), ('lon', 'lat'), split...  14.2 us
    all_to_all x1, starting transfers between devices, per_device(): lax.all_to_all(sent.reshape(ndev, capacity, LANES), ('lon', 'lat'), split...  12.2 us
    all_to_all x1, waiting for transfers between devices, per_device(): lax.all_to_all(field, 'lon', split_axis=0, concat_axis=0, tiled=True)  11.6 us
    pallas_call x1, Pallas kernels, call_convolve(): pl.pallas_call(conv_kernel, out_shape=jax.ShapeDtypeStruct(coded, I16), i...  7.8 us
    pallas_call x1, Pallas kernels, per_device(): pl.pallas_call(lambda *refs: prepare_kernel(lat_dev, *refs), out_shape=(j...  5.93 us
    pallas_call x1, Pallas kernels, per_device(): pl.pallas_call(lambda *refs: dispatch_kernel(capacity, *refs), out_shape=...  5.76 us
  transfers between devices with their start and end apart: 2, of which 2 were waited for; matrix products, arithmetic and copies ran while one was open for 3% of the time, Pallas kernels for 7%

profile of v9, /device:TPU:1, one launch (start us, length us, event | category | flops | bytes accessed | tf_op | source)
XLA Modules:
  0.0 121.9 jit_solution(7161009957752156641)
XLA Ops:
  0.7 5.8 %dispatch.1 = bf16[5120,128]{1,0:T(8,128)(2,1)} custom-call(s32[1]{0:T(128)S(6)} %copy.10.refs_0_, bf16[2048,128]{1,0:T(8,128)(2,1)} %refs_1_.1, s32[1,2048]{1,0:T(1,128)} %bitcast.15, s32[4,2048]{1,0:T(4,128)} %bitcast.11, s32[1,2048]{1,0:T(1,128)} %bitcast.16, bf16[96,128]{1,0:T(8,128)(2,1)} %bitcast.13), custom_call_target="tpu_custom_call" | custom-call | tf_op jit(solution)/shard_map/dispatch/pallas_call | solution.py:480
  6.4 12.2 %all-to-all-start = ((bf16[128,40,128]{2,1,0:T(8,128)(2,1)}), bf16[128,40,128]{2,1,0:T(8,128)(2,1)}, u32[]{:S(2)}, u32[]{:S(2)}) async-start(bf16[128,40,128]{2,1,0:T(8,128)(2,1)} %bitcast.9), calls=%async_computation | async-start | bytes 2621440 | tf_op jit(solution)/shard_map/all_to_all | solution.py:504
  18.6 5.9 %prepare.1 = (f32[6144,128]{1,0:T(8,128)}, bf16[256,256]{1,0:T(8,128)(2,1)}) custom-call(f32[6144,96]{1,0:T(8,128)} %bitcast.10, f32[96,96]{1,0:T(8,128)} %refs_1_.2), custom_call_target="tpu_custom_call" | custom-call | bytes 12000000 | tf_op jit(solution)/shard_map/prepare/pallas_call | solution.py:507
  24.5 14.2 %all-to-all-done = bf16[128,40,128]{2,1,0:T(8,128)(2,1)} async-done(((bf16[128,40,128]{2,1,0:T(8,128)(2,1)}), bf16[128,40,128]{2,1,0:T(8,128)(2,1)}, u32[]{:S(2)}, u32[]{:S(2)}) %all-to-all-start) | async-done | bytes 1310752 | tf_op jit(solution)/shard_map/all_to_all | solution.py:504
  38.7 24.2 %spread.1 = s16[16,104,384]{2,1,0:T(8,128)(2,1)} custom-call(bf16[5120,128]{1,0:T(8,128)(2,1)} %bitcast.5.refs_0_, f32[6144,128]{1,0:T(8,128)} %get-tuple-element.17.refs_1_, bf16[256,256]{1,0:T(8,128)(2,1)} %get-tuple-element.18.refs_2_), custom_call_target="tpu_custom_call" | custom-call | tf_op jit(solution)/shard_map/spread/pallas_call | solution.py:398
  62.9 0.0 copy-start
  62.9 5.0 %all-to-all-start.1 = ((s16[16,104,384]{2,1,0:T(8,128)(2,1)}), s16[16,104,384]{2,1,0:T(8,128)(2,1)}, u32[]{:S(2)}, u32[]{:S(2)}) async-start(s16[16,104,384]{2,1,0:T(8,128)(2,1)} %spread.1), calls=%async_computation.1 | async-start | bytes 2555904 | tf_op jit(solution)/shard_map/all_to_all | solution.py:537
  67.9 0.0 copy-done
  67.9 0.6 slice.41
  68.5 0.1 slice.42
  68.6 0.1 fusion.1
  68.6 0.5 slice.49
  69.2 0.1 slice.50
  69.2 0.1 reverse.6
  69.3 0.1 slice.55
  69.4 0.1 slice.46
  69.5 0.8 fusion
  70.3 0.1 reverse.5
  70.3 0.1 slice.54
  70.4 0.7 pad_maximum_fusion.2
  71.1 0.6 pad_maximum_fusion.kern_ref
  71.7 3.1 %toeplitz.1 = (bf16[768,768]{1,0:T(8,128)(2,1)}, bf16[768,768]{1,0:T(8,128)(2,1)}, bf16[768,768]{1,0:T(8,128)(2,1)}, bf16[768,768]{1,0:T(8,128)(2,1)}) custom-call(f32[2,768]{1,0:T(2,128)} %pad_maximum_fusion.kern_ref), custom_call_target="tpu_custom_call" | custom-call | tf_op jit(solution)/shard_map/toeplitz/pallas_call | solution.py:528
  74.8 11.6 %all-to-all-done.1.refs_0_ = s16[16,104,384]{2,1,0:T(8,128)(2,1)} async-done(((s16[16,104,384]{2,1,0:T(8,128)(2,1)}), s16[16,104,384]{2,1,0:T(8,128)(2,1)}, u32[]{:S(2)}, u32[]{:S(2)}) %all-to-all-start.1) | async-done | bytes 1277984 | tf_op jit(solution)/shard_map/all_to_all | solution.py:537
  86.4 7.8 %convolve.1 = s16[16,104,384]{2,1,0:T(8,128)(2,1)} custom-call(s16[16,104,384]{2,1,0:T(8,128)(2,1)} %all-to-all-done.1.refs_0_, bf16[768,768]{1,0:T(8,128)(2,1)} %get-tuple-element.19.refs_1_, bf16[768,768]{1,0:T(8,128)(2,1)} %get-tuple-element.20.refs_2_, bf16[768,768]{1,0:T(8,128)(2,1)} %get-tuple-element.21.refs_3_, ...), custom_call_target="tpu_custom_call" | custom-call | tf_op jit(solution)/shard_map/convolve/pallas_call | solution.py:425
  94.2 23.3 %all_to_all.15.got_ref = s16[16,104,384]{2,1,0:T(8,128)(2,1)} all-to-all(s16[16,104,384]{2,1,0:T(8,128)(2,1)} %convolve.1), channel_id=1, replica_groups=mesh['lon'=16,'lat'=8] {'lon'}, dimensions={0} | all-to-all | bytes 2555904 | tf_op jit(solution)/shard_map/all_to_all | solution.py:539
  117.6 4.3 %unpack.1 = f32[96,64,96]{2,1,0:T(8,128)} custom-call(s16[16,104,384]{2,1,0:T(8,128)(2,1)} %all_to_all.15.got_ref), custom_call_target="tpu_custom_call" | custom-call | tf_op jit(solution)/shard_map/unpack/pallas_call | solution.py:447
  (2 shorter events, 0.0 us)
Async XLA Ops:
  6.4 32.3 %all-to-all-start = ((bf16[128,40,128]{2,1,0:T(8,128)(2,1)}), bf16[128,40,128]{2,1,0:T(8,128)(2,1)}, u32[]{:S(2)}, u32[]{:S(2)}) async-start(bf16[128,40,128]{2,1,0:T(8,128)(2,1)} %bitcast.9), calls=%async_computation | async-start | bytes 2621440 | tf_op jit(solution)/shard_map/all_to_all | solution.py:504
  62.9 5.0 %copy-start = (f32[1536]{0:T(1024)S(1)}, f32[1536]{0:T(1024)}, u32[]{:S(2)}) copy-start(f32[1536]{0:T(1024)} %param.17) | copy-start | bytes 18436
  62.9 23.5 %all-to-all-start.1 = ((s16[16,104,384]{2,1,0:T(8,128)(2,1)}), s16[16,104,384]{2,1,0:T(8,128)(2,1)}, u32[]{:S(2)}, u32[]{:S(2)}) async-start(s16[16,104,384]{2,1,0:T(8,128)(2,1)} %spread.1), calls=%async_computation.1 | async-start | bytes 2555904 | tf_op jit(solution)/shard_map/all_to_all | solution.py:537
